TPU v7x, 32 devices: a whole 2x2x4 slice. The times are simulated.
32 devices in a mesh: dp: 4 (over x, core), sector: 8 (over z, y).
Axes of the slice: x: 2, y: 2, z: 4, core: 2. Of those that a mesh axis runs over, the one named last changes fastest.
Arguments:
- hits: bfloat16 [4, 16384, 256], P('dp', 'sector'), may hold values from -6 to 6
- tiles: bfloat16 [4, 128, 8, 128, 128], P('dp', 'sector'), may hold values from -0.1875 to 0.1875
- sources: int32 [4, 128, 8], P('dp', 'sector'), may hold values from 0 to 23
- send_list: int32 [4, 8, 2, 4], P('dp'), may hold values from 0 to 15, as said below
- w_message: bfloat16 [2, 256, 256], replicated, may hold values from -0.375 to 0.375
- w_self: bfloat16 [2, 256, 256], replicated, may hold values from -0.375 to 0.375
- cotangent: float32 [4, 16384, 256], P('dp', 'sector'), may hold values from -6 to 6
Outputs:
- hit_output: bfloat16 [4, 16384, 256], P('dp', 'sector')
- hit_grad: float32 [4, 16384, 256], P('dp', 'sector')
- message_grad: float32 [2, 256, 256], replicated
- self_grad: float32 [2, 256, 256], replicated
Inputs may be any that keep to these rules, and one draw needn't show every extreme that they name: `send_list`: each list holds 4 distinct local block numbers of its sector.
All inputs are finite; a program needn't handle non-finite values.
Results may differ from a plain program's by a relative error of at most 0.007.
Values may be sent and summed in bfloat16 or wider, within the bound.
A program may use at most 128 MiB of HBM per device.

v0:
```python
import jax
import jax.numpy as jnp
from jax import lax
from jax.sharding import PartitionSpec as P

LAYERS = 2


def extended_2(cells, sides, width):
    for axis, dim in sides:
        count = lax.axis_size(axis)
        head = lax.slice_in_dim(cells, 0, width, axis=dim)
        tail = lax.slice_in_dim(cells, cells.shape[dim] - width, cells.shape[dim], axis=dim)
        cells = jnp.concatenate(
            [
                lax.ppermute(tail, axis, [(i, (i + 1) % count) for i in range(count)]),
                cells,
                lax.ppermute(head, axis, [((i + 1) % count, i) for i in range(count)]),
            ],
            axis=dim,
        )
    return cells


def silu_grad(pre):
    sig = jax.nn.sigmoid(pre)
    return sig * (1.0 + pre * (1.0 - sig))


def per_device(hits, tiles, sources, send_list, w_message, w_self, cotangent):
    blocks_here = tiles.shape[1]
    tile_rows = tiles.shape[3]
    width = hits.shape[2]
    lent = send_list.shape[3]
    listed = tiles.shape[2]
    sector_here = lax.axis_index("sector")
    lists = send_list[0]
    own_lists = lax.dynamic_index_in_dim(lists, sector_here, 0, keepdims=False)
    tile_data = tiles[0]
    slot_ids = sources[0]
    slot_count = blocks_here + 2 * lent
    flat_ids = slot_ids.reshape(-1)
    current = hits[0]
    saved = []
    for layer_index in range(LAYERS):
        message = jnp.dot(
            current, w_message[layer_index], preferred_element_type=jnp.float32
        ).astype(jnp.bfloat16)
        message_blocks = message.reshape(blocks_here, tile_rows, width)
        packet = jnp.concatenate(
            [message_blocks[own_lists[1]], message_blocks[own_lists[0]]]
        ).reshape(2 * lent * tile_rows, width)
        extended = extended_2(packet, (("sector", 0),), lent * tile_rows)
        table = jnp.concatenate(
            [
                message_blocks,
                extended[: lent * tile_rows].reshape(lent, tile_rows, width),
                extended[-lent * tile_rows :].reshape(lent, tile_rows, width),
            ]
        )
        gathered = table[slot_ids]
        aggregate = jnp.einsum(
            "bkij,bkjf->bif", tile_data, gathered, preferred_element_type=jnp.float32
        )
        pre = aggregate.reshape(-1, width) + jnp.dot(
            current, w_self[layer_index], preferred_element_type=jnp.float32
        )
        saved.append((current, pre))
        current = (current.astype(jnp.float32) + jax.nn.silu(pre)).astype(jnp.bfloat16)
    grad = cotangent[0]
    message_steps = [None] * LAYERS
    self_steps = [None] * LAYERS
    for layer_index in reversed(range(LAYERS)):
        layer_in, pre = saved[layer_index]
        dpre = (grad * silu_grad(pre)).astype(jnp.bfloat16)
        contrib = jnp.einsum(
            "bkij,bif->bkjf",
            tile_data,
            dpre.reshape(blocks_here, tile_rows, width),
            preferred_element_type=jnp.float32,
        )
        slot_grad = jax.ops.segment_sum(
            contrib.reshape(blocks_here * listed, tile_rows * width),
            flat_ids,
            num_segments=slot_count,
        )
        packet = slot_grad[blocks_here:].reshape(2 * lent * tile_rows, width)
        extended = extended_2(packet, (("sector", 0),), lent * tile_rows)
        dblocks = slot_grad[:blocks_here].reshape(blocks_here, tile_rows, width)
        dblocks = dblocks.at[own_lists[1]].add(
            extended[: lent * tile_rows].reshape(lent, tile_rows, width)
        )
        dblocks = dblocks.at[own_lists[0]].add(
            extended[-lent * tile_rows :].reshape(lent, tile_rows, width)
        )
        dmessage = dblocks.reshape(-1, width).astype(jnp.bfloat16)
        self_part = jnp.dot(layer_in.T, dpre, preferred_element_type=jnp.float32)
        message_part = jnp.dot(layer_in.T, dmessage, preferred_element_type=jnp.float32)
        message_steps[layer_index] = message_part
        self_steps[layer_index] = self_part
        grad = grad + jnp.dot(dpre, w_self[layer_index].T, preferred_element_type=jnp.float32)
        grad = grad + jnp.dot(
            dmessage, w_message[layer_index].T, preferred_element_type=jnp.float32
        )
    message_total = jnp.stack(message_steps)
    self_total = jnp.stack(self_steps)
    message_total, self_total = lax.psum((message_total, self_total), ("dp", "sector"))
    total_rows = blocks_here * tile_rows * lax.axis_size(("dp", "sector"))
    scale = 1.0 / jnp.sqrt(jnp.float32(total_rows))
    return (current[None], grad[None], message_total * scale, self_total * scale)


def solution(mesh):
    in_specs = (
        P("dp", "sector", None),
        P("dp", "sector", None, None, None),
        P("dp", "sector", None),
        P("dp", None, None, None),
        P(),
        P(),
        P("dp", "sector", None),
    )
    out_specs = (P("dp", "sector", None), P("dp", "sector", None), P(), P())
    return jax.shard_map(
        per_device, mesh=mesh, in_specs=in_specs, out_specs=out_specs, check_vma=False
    )
```

profile of v0, /device:TPU:1, one launch (start us, length us, event | category | flops | bytes accessed | tf_op | source)
XLA Modules:
  0.0 399.9 jit_solution(3526212417118302410)
XLA Ops:
  10.4 2.1 collective-permute-start
  13.1 3.1 collective-permute-start.1
  16.4 6.7 %collective-permute-done = bf16[512,256]{1,0:T(8,128)(2,1)S(1)} collective-permute-done((bf16[512,256]{1,0:T(8,128)(2,1)S(1)}, bf16[512,256]{1,0:T(8,128)(2,1)S(1)}, u32[]{:S(2)}, u32[]{:S(2)}) %collective-permute-start) | collective-permute-done | bytes 262176 | tf_op jit(solution)/shard_map/ppermute | solution.py:16
  23.1 2.9 collective-permute-done.1
  26.2 6.6 %gather_fusion.2 = bf16[128,128,256]{2,1,0:T(8,128)(2,1)} fusion(bf16[24,128,256]{2,1,0:T(8,128)(2,1)S(1)} %pad_maximum_fusion, s32[1024]{0:T(1024)S(1)} %pad_clamp_fusion), kind=kCustom, calls=%fused_computation.2 | custom fusion | bytes 16777728 | tf_op jit(solution)/shard_map/gather | solution.py:61
  32.8 6.3 %fusion.2 = f32[16,256,128,1]{1,2,3,0:T(8,128)S(1)} fusion(bf16[16,8,128,256]{3,2,1,0:T(8,128)(2,1)} %bitcast.151, bf16[1,16,8,128,128]{4,3,2,1,0:T(8,128)(2,1)} %param.8), kind=kOutput, calls=%fused_computation.16 | convolution fusion | flops 1073741824 | bytes 14680064 | tf_op jit(solution)/shard_map/bkij,bkjf->bif/dot_general | solution.py:62
  39.1 2.1 add_convert_fusion.1
  43.9 4.3 %collective-permute-start.3 = (bf16[512,256]{1,0:T(8,128)(2,1)S(1)}, bf16[512,256]{1,0:T(8,128)(2,1)S(1)}, u32[]{:S(2)}, u32[]{:S(2)}) collective-permute-start(bf16[512,256]{1,0:T(8,128)(2,1)S(1)} %bitcast.179), channel_id=1, source_target_pairs={{1,0},{2,1},{3,2},{4,3},{5,4},{6,5},{7,6},{0,7},{9,8},{10,9},{11,1... | collective-permute-start | bytes 786440 | tf_op jit(solution)/shard_map/ppermute | solution.py:18
  48.4 4.5 %collective-permute-done.2 = bf16[512,256]{1,0:T(8,128)(2,1)S(1)} collective-permute-done((bf16[512,256]{1,0:T(8,128)(2,1)S(1)}, bf16[512,256]{1,0:T(8,128)(2,1)S(1)}, u32[]{:S(2)}, u32[]{:S(2)}) %collective-permute-start.2) | collective-permute-done | bytes 262176 | tf_op jit(solution)/shard_map/ppermute | solution.py:16
  52.9 5.2 %collective-permute-done.3 = bf16[512,256]{1,0:T(8,128)(2,1)S(1)} collective-permute-done((bf16[512,256]{1,0:T(8,128)(2,1)S(1)}, bf16[512,256]{1,0:T(8,128)(2,1)S(1)}, u32[]{:S(2)}, u32[]{:S(2)}) %collective-permute-start.3) | collective-permute-done | bytes 262176 | tf_op jit(solution)/shard_map/ppermute | solution.py:18
  58.3 6.6 %gather_fusion.5 = bf16[128,128,256]{2,1,0:T(8,128)(2,1)} fusion(bf16[24,128,256]{2,1,0:T(8,128)(2,1)S(1)} %pad_maximum_fusion.1, s32[1024]{0:T(1024)S(1)} %pad_clamp_fusion), kind=kCustom, calls=%fused_computation.5 | custom fusion | bytes 16777728 | tf_op jit(solution)/shard_map/gather | solution.py:61
  64.9 6.3 %fusion.4 = f32[16,256,128,1]{1,2,3,0:T(8,128)S(1)} fusion(bf16[16,8,128,256]{3,2,1,0:T(8,128)(2,1)} %bitcast.150, bf16[1,16,8,128,128]{4,3,2,1,0:T(8,128)(2,1)} %param.8), kind=kOutput, calls=%fused_computation.18 | convolution fusion | flops 1073741824 | bytes 14680064 | tf_op jit(solution)/shard_map/bkij,bkjf->bif/dot_general | solution.py:62
  71.2 2.3 fusion.7
  74.5 8.1 %convolution_bitcast_fusion.1 = f32[16,8,128,256]{2,3,1,0:T(8,128)} fusion(bf16[16,128,256,1]{2,1,3,0:T(8,128)(2,1)S(1)} %bitcast.161, bf16[1,16,8,128,128]{4,3,2,1,0:T(8,128)(2,1)S(1)} %copy-done), kind=kOutput, calls=%fused_computation.13 | convolution fusion | flops 1073741824 | bytes 22020096 | tf_op jit(solution)/shard_map/bkij,bif->bkjf/dot_general | solution.py:76
  82.6 17.7 %copy.39 = f32[16,8,128,256]{3,1,2,0:T(8,128)} copy(f32[16,8,128,256]{2,3,1,0:T(8,128)} %convolution_bitcast_fusion.1) | data formatting | bytes 33554432
  100.3 24.9 %scatter_custom_fusion = f32[24,32768]{1,0:T(8,128)S(1)} fusion(s32[128]{0:T(128)S(1)} %reshape.238, f32[128,32768]{1,0:T(8,128)} %bitcast.153, f32[]{:T(128)} %constant.24.clone.1), kind=kCustom, calls=%fused_computation.40 | custom fusion | flops 4194304 | bytes 3146240 | tf_op jit(solution)/shard_map/scatter-add | solution.py:82
  127.1 2.3 slice.96
  129.4 2.2 slice.94
  131.6 4.2 %collective-permute-start.5 = (f32[512,256]{1,0:T(8,128)}, f32[512,256]{1,0:T(8,128)}, u32[]{:S(2)}, u32[]{:S(2)}) collective-permute-start(f32[512,256]{1,0:T(8,128)} %slice.96), channel_id=1, source_target_pairs={{1,0},{2,1},{3,2},{4,3},{5,4},{6,5},{7,6},{0,7},{9,8},{10,9},{11,1... | collective-permute-start | bytes 1572872 | tf_op jit(solution)/shard_map/ppermute | solution.py:18
  135.7 2.4 convolution_bitcast_fusion.2
  140.0 13.3 %collective-permute-done.4 = f32[512,256]{1,0:T(8,128)S(1)} collective-permute-done((f32[512,256]{1,0:T(8,128)}, f32[512,256]{1,0:T(8,128)S(1)}, u32[]{:S(2)}, u32[]{:S(2)}) %collective-permute-start.4) | collective-permute-done | bytes 524320 | tf_op jit(solution)/shard_map/ppermute | solution.py:16
  161.6 4.0 multiply_convert_fusion
  165.6 8.1 %convolution_bitcast_fusion = f32[16,8,128,256]{2,3,1,0:T(8,128)} fusion(bf16[16,128,256,1]{2,1,3,0:T(8,128)(2,1)S(1)} %bitcast.154, bf16[1,16,8,128,128]{4,3,2,1,0:T(8,128)(2,1)S(1)} %copy-done.1), kind=kOutput, calls=%fused_computation.12 | convolution fusion | flops 1073741824 | bytes 22020096 | tf_op jit(solution)/shard_map/bkij,bif->bkjf/dot_general | solution.py:76
  173.7 17.6 %copy.41 = f32[16,8,128,256]{3,1,2,0:T(8,128)} copy(f32[16,8,128,256]{2,3,1,0:T(8,128)} %convolution_bitcast_fusion) | data formatting | bytes 33554432
  191.3 25.8 %scatter_custom_fusion.3 = f32[24,32768]{1,0:T(8,128)} fusion(s32[128]{0:T(128)S(1)} %reshape.238, f32[128,32768]{1,0:T(8,128)} %bitcast.152, f32[]{:T(128)} %constant.24.clone.1), kind=kCustom, calls=%fused_computation.38 | custom fusion | flops 4194304 | bytes 3146240 | tf_op jit(solution)/shard_map/scatter-add | solution.py:82
  217.1 2.7 fusion.35
  222.1 2.2 slice.101
  224.3 2.2 slice.99
  226.8 3.9 collective-permute-start.7
  234.4 13.1 %collective-permute-done.6 = f32[512,256]{1,0:T(8,128)S(1)} collective-permute-done((f32[512,256]{1,0:T(8,128)}, f32[512,256]{1,0:T(8,128)S(1)}, u32[]{:S(2)}, u32[]{:S(2)}) %collective-permute-start.6) | collective-permute-done | bytes 524320 | tf_op jit(solution)/shard_map/ppermute | solution.py:16
  250.2 2.5 collective-permute-done.7
  261.2 128.3 %all-reduce.3.cloned.1.call-done = (f32[2,256,256]{1,2,0:T(8,128)}, f32[2,256,256]{1,2,0:T(8,128)}) async-done(((f32[2,256,256]{1,2,0:T(8,128)}, f32[2,256,256]{1,2,0:T(8,128)}), (f32[2,256,256]{1,2,0:T(8,128)}, f32[2,256,256]{1,2,0:T(8,128)})) %all-reduce.3.cloned.1.call-update) | async-done | bytes 1048592 | tf_op jit(solution)/shard_map/psum | solution.py:107
  (102 shorter events, 40.6 us)
Async XLA Ops:
  7.2 9.0 %copy-start.26 = (s32[1,16,8]{1,2,0:T(8,128)S(1)}, s32[1,16,8]{1,2,0:T(8,128)}, u32[]{:S(2)}) copy-start(s32[1,16,8]{1,2,0:T(8,128)} %param.9) | copy-start | bytes 1540
  7.2 382.3 %all-reduce.3.cloned.1.call-start = ((), (), s32[]{:S(2)}) async-start(), calls=%async_computation | async-start | bytes 2097152 | tf_op jit(solution)/shard_map/psum | solution.py:107
  10.4 12.7 %collective-permute-start = (bf16[512,256]{1,0:T(8,128)(2,1)S(1)}, bf16[512,256]{1,0:T(8,128)(2,1)S(1)}, u32[]{:S(2)}, u32[]{:S(2)}) collective-permute-start(bf16[512,256]{1,0:T(8,128)(2,1)S(1)} %bitcast.178), channel_id=1, source_target_pairs={{0,1},{1,2},{2,3},{3,4},{4,5},{5,6},{6,7},{7,0},{8,9},{9,10},{10,1... | collective-permute-start | bytes 786440 | tf_op jit(solution)/shard_map/ppermute | solution.py:16
  13.1 12.9 %collective-permute-start.1 = (bf16[512,256]{1,0:T(8,128)(2,1)S(1)}, bf16[512,256]{1,0:T(8,128)(2,1)S(1)}, u32[]{:S(2)}, u32[]{:S(2)}) collective-permute-start(bf16[512,256]{1,0:T(8,128)(2,1)S(1)} %bitcast.180), channel_id=1, source_target_pairs={{1,0},{2,1},{3,2},{4,3},{5,4},{6,5},{7,6},{0,7},{9,8},{10,9},{11,1... | collective-permute-start | bytes 786440 | tf_op jit(solution)/shard_map/ppermute | solution.py:18
  32.8 6.3 %copy-start.2 = (bf16[1,2048,256]{2,1,0:T(8,128)(2,1)S(1)}, bf16[1,2048,256]{2,1,0:T(8,128)(2,1)}, u32[]{:S(2)}) copy-start(bf16[1,2048,256]{2,1,0:T(8,128)(2,1)} %param.7) | copy-start | bytes 3145732
  32.8 6.3 %copy-start.23 = (bf16[2,256,256]{2,1,0:T(8,128)(2,1)S(1)}, bf16[2,256,256]{2,1,0:T(8,128)(2,1)}, u32[]{:S(2)}) copy-start(bf16[2,256,256]{2,1,0:T(8,128)(2,1)} %param.12) | copy-start | bytes 786436
  39.1 3.1 copy-start.17
  43.8 9.1 %collective-permute-start.2 = (bf16[512,256]{1,0:T(8,128)(2,1)S(1)}, bf16[512,256]{1,0:T(8,128)(2,1)S(1)}, u32[]{:S(2)}, u32[]{:S(2)}) collective-permute-start(bf16[512,256]{1,0:T(8,128)(2,1)S(1)} %bitcast.181), channel_id=1, source_target_pairs={{0,1},{1,2},{2,3},{3,4},{4,5},{5,6},{6,7},{7,0},{8,9},{9,10},{10,1... | collective-permute-start | bytes 786440 | tf_op jit(solution)/shard_map/ppermute | solution.py:16
  43.9 14.2 %collective-permute-start.3 = (bf16[512,256]{1,0:T(8,128)(2,1)S(1)}, bf16[512,256]{1,0:T(8,128)(2,1)S(1)}, u32[]{:S(2)}, u32[]{:S(2)}) collective-permute-start(bf16[512,256]{1,0:T(8,128)(2,1)S(1)} %bitcast.179), channel_id=1, source_target_pairs={{1,0},{2,1},{3,2},{4,3},{5,4},{6,5},{7,6},{0,7},{9,8},{10,9},{11,1... | collective-permute-start | bytes 786440 | tf_op jit(solution)/shard_map/ppermute | solution.py:18
  64.9 6.3 %copy-start.8 = (f32[1,2048,256]{2,1,0:T(8,128)S(1)}, f32[1,2048,256]{2,1,0:T(8,128)}, u32[]{:S(2)}) copy-start(f32[1,2048,256]{2,1,0:T(8,128)} %param.13) | copy-start | bytes 6291460
  64.9 6.3 %copy-start.15 = (bf16[2048,256]{1,0:T(8,128)(2,1)S(1)}, bf16[2048,256]{1,0:T(8,128)(2,1)}, u32[]{:S(2)}) copy-start(bf16[2048,256]{1,0:T(8,128)(2,1)} %copy-done.14) | copy-start | bytes 3145732
  64.9 6.3 %copy-start.24 = (bf16[2,256,256]{2,1,0:T(8,128)(2,1)S(1)}, bf16[2,256,256]{2,1,0:T(8,128)(2,1)}, u32[]{:S(2)}) copy-start(bf16[2,256,256]{2,1,0:T(8,128)(2,1)} %param.12) | copy-start | bytes 786436
  71.2 3.3 copy-start
  127.1 8.7 %copy-start.7 = (bf16[2048,256]{1,0:T(8,128)(2,1)S(1)}, bf16[2048,256]{1,0:T(8,128)(2,1)}, u32[]{:S(2)}) copy-start(bf16[2048,256]{1,0:T(8,128)(2,1)} %copy-done.6) | copy-start | bytes 3145732
  131.6 6.6 %copy-start.9 = (f32[1,2048,256]{2,1,0:T(8,128)S(1)}, f32[1,2048,256]{2,1,0:T(8,128)}, u32[]{:S(2)}) copy-start(f32[1,2048,256]{2,1,0:T(8,128)} %param.13) | copy-start | bytes 6291460
  131.6 6.6 %copy-start.25 = (bf16[2,256,256]{2,1,0:T(8,128)(2,1)S(1)}, bf16[2,256,256]{2,1,0:T(8,128)(2,1)}, u32[]{:S(2)}) copy-start(bf16[2,256,256]{2,1,0:T(8,128)(2,1)} %param.12) | copy-start | bytes 786436
  131.6 21.7 %collective-permute-start.4 = (f32[512,256]{1,0:T(8,128)}, f32[512,256]{1,0:T(8,128)S(1)}, u32[]{:S(2)}, u32[]{:S(2)}) collective-permute-start(f32[512,256]{1,0:T(8,128)} %slice.94), channel_id=1, source_target_pairs={{0,1},{1,2},{2,3},{3,4},{4,5},{5,6},{6,7},{7,0},{8,9},{9,10},{10,1... | collective-permute-start | bytes 1572872 | tf_op jit(solution)/shard_map/ppermute | solution.py:16
  131.6 26.1 %collective-permute-start.5 = (f32[512,256]{1,0:T(8,128)}, f32[512,256]{1,0:T(8,128)}, u32[]{:S(2)}, u32[]{:S(2)}) collective-permute-start(f32[512,256]{1,0:T(8,128)} %slice.96), channel_id=1, source_target_pairs={{1,0},{2,1},{3,2},{4,3},{5,4},{6,5},{7,6},{0,7},{9,8},{10,9},{11,1... | collective-permute-start | bytes 1572872 | tf_op jit(solution)/shard_map/ppermute | solution.py:18
  159.6 2.0 copy-start.11
  159.8 5.8 %copy-start.12 = (bf16[16,128,256]{2,1,0:T(8,128)(2,1)}, bf16[16,128,256]{2,1,0:T(8,128)(2,1)S(1)}, u32[]{:S(2)}) copy-start(bf16[16,128,256]{2,1,0:T(8,128)(2,1)S(1)} %convert_element_type.45) | copy-start | bytes 3145732
  161.6 4.0 copy-start.1
  219.9 1.6 slice-start
  226.5 5.9 %copy-start.21 = (f32[1,256,256]{1,2,0:T(8,128)S(1)}, f32[1,256,256]{1,2,0:T(8,128)}, u32[]{:S(2)}) copy-start(f32[1,256,256]{1,2,0:T(8,128)} %convolution_bitcast_fusion.2) | copy-start | bytes 786436
  226.5 6.7 %copy-start.13 = (bf16[16,128,256]{2,1,0:T(8,128)(2,1)S(1)}, bf16[16,128,256]{2,1,0:T(8,128)(2,1)}, u32[]{:S(2)}) copy-start(bf16[16,128,256]{2,1,0:T(8,128)(2,1)} %copy-done.12) | copy-start | bytes 3145732
  226.5 6.7 %copy-start.16 = (bf16[2048,256]{1,0:T(8,128)(2,1)S(1)}, bf16[2048,256]{1,0:T(8,128)(2,1)}, u32[]{:S(2)}) copy-start(bf16[2048,256]{1,0:T(8,128)(2,1)} %copy-done.14) | copy-start | bytes 3145732
  226.5 21.1 %collective-permute-start.6 = (f32[512,256]{1,0:T(8,128)}, f32[512,256]{1,0:T(8,128)S(1)}, u32[]{:S(2)}, u32[]{:S(2)}) collective-permute-start(f32[512,256]{1,0:T(8,128)} %slice.99), channel_id=1, source_target_pairs={{0,1},{1,2},{2,3},{3,4},{4,5},{5,6},{6,7},{7,0},{8,9},{9,10},{10,1... | collective-permute-start | bytes 1572872 | tf_op jit(solution)/shard_map/ppermute | solution.py:16
  226.8 25.9 %collective-permute-start.7 = (f32[512,256]{1,0:T(8,128)}, f32[512,256]{1,0:T(8,128)}, u32[]{:S(2)}, u32[]{:S(2)}) collective-permute-start(f32[512,256]{1,0:T(8,128)} %slice.101), channel_id=1, source_target_pairs={{1,0},{2,1},{3,2},{4,3},{5,4},{6,5},{7,6},{0,7},{9,8},{10,9},{11,1... | collective-permute-start | bytes 1572872 | tf_op jit(solution)/shard_map/ppermute | solution.py:18
  254.6 1.6 copy-start.3
  254.6 2.1 copy-start.22
  254.7 1.9 copy-start.4
  256.2 1.7 copy-start.10
  389.5 2.1 copy-start.18
  (5 other events, 5.0 us)
Sparse Core Ops, SparseCore 0:
  257.6 131.7 all-reduce.2
where the time goes:
time: 407 us; the launch traced here: 400 us
  waiting for transfers between devices  178 us (44%)
  local copies, waits for them, and re-layouts  77 us (19%)
  other arithmetic  61.7 us (15%)
  matrix products  50.2 us (12%)
  starting transfers between devices  18 us (4%)
  between operations  14.9 us (4%)
    psum x1, waiting for transfers between devices, per_device(): lax.psum((message_total, self_total), ('dp', 'sector'))  128 us
    scatter-add x2, other arithmetic, per_device(): jax.ops.segment_sum(contrib.reshape(blocks_here * listed, tile_rows * wid...  50.7 us
    unnamed x61, local copies, waits for them, and re-layouts  45.9 us
    ppermute x4, waiting for transfers between devices, extended_2(): lax.ppermute(tail, axis, [(i, (i + 1) % count) for i in range(count)])  37.6 us
    dot_general x2, matrix products, per_device(): jnp.einsum('bkij,bif->bkjf', tile_data, dpre.reshape(blocks_here, tile_ro...  16.2 us
    ppermute x4, starting transfers between devices, extended_2(): lax.ppermute(head, axis, [((i + 1) % count, i) for i in range(count)])  15.5 us
    gather x2, local copies, waits for them, and re-layouts, per_device(): gathered = table[slot_ids]  13.2 us
    dot_general x2, matrix products, per_device(): jnp.einsum('bkij,bkjf->bif', tile_data, gathered, preferred_element_type=...  12.6 us
  transfers between devices with their start and end apart: 9, of which 9 were waited for; matrix products, arithmetic and copies ran while one was open for 4% of the time, Pallas kernels for 0%

commit v1 on v0

v1 whole, which is shorter than its diff:
```python
import functools

import jax
import jax.numpy as jnp
from jax import lax
from jax.experimental import pallas as pl
from jax.experimental.pallas import tpu as pltpu
from jax.sharding import PartitionSpec as P

LAYERS = 2
CHUNK = 256
BF = jnp.bfloat16
F32 = jnp.float32
MESH = pl.DeviceIdType.MESH


def mm(a, b):
    return lax.dot_general(a, b, (((1,), (0,)), ((), ())), preferred_element_type=F32)


def mm_bt(a, b):
    return lax.dot_general(a, b, (((1,), (1,)), ((), ())), preferred_element_type=F32)


def silu_grad(pre):
    sig = jax.nn.sigmoid(pre)
    return sig * (1.0 + pre * (1.0 - sig))


def kernel(
    ndp, nsec, blocks, listed, lent, tile, width, r1, r2,
    pick_ref, lists_ref, back_pos, back_on, hits_hbm, tiles_hbm, cot_hbm, wm_ref, ws_ref,
    hit_out, grad_out, mg_out, sg_out,
    h0, h1, h2, tiles, g, pre0, pre1, msg, a_own, a_halo, halo, lend,
    dpre, dpre_t, dmsg_t, own_t, back_send, back_recv0, back_recv1,
    part, rs1, q1, rs2, r_own, g2, g1,
    load_sem, store_sem, halo_ss, halo_rs, back_ss, back_rs,
    rs1_ss, rs1_rs, rs2_ss, rs2_rs, ag2_ss, ag2_rs, ag1_ss, ag1_rs,
):
    back_recv = (back_recv0, back_recv1)
    rows = blocks * tile
    chunks = rows // CHUNK
    per_chunk = CHUNK // tile
    dp = lax.axis_index("dp")
    sec = lax.axis_index("sector")
    upper = lax.rem(sec + 1, nsec)
    lower = lax.rem(sec + nsec - 1, nsec)
    sec_peers = [lax.rem(sec + o, nsec) for o in range(1, nsec)]
    dp_peers = [lax.rem(dp + o, ndp) for o in range(1, ndp)]
    owners = r1 // r2

    loads = [
        pltpu.make_async_copy(hits_hbm, h0, load_sem.at[0]),
        pltpu.make_async_copy(tiles_hbm, tiles, load_sem.at[1]),
        pltpu.make_async_copy(cot_hbm, g, load_sem.at[2]),
    ]
    for c in loads:
        c.start()

    barrier = pltpu.get_barrier_semaphore()
    for p in sec_peers:
        pl.semaphore_signal(barrier, inc=1, device_id=(dp, p), device_id_type=MESH)
    for p in dp_peers:
        pl.semaphore_signal(barrier, inc=1, device_id=(p, sec), device_id_type=MESH)

    def cond(flag, fn):
        if owners == nsec:
            fn()
        else:
            pl.when(flag)(fn)

    def remote(src, dst, ss, rs, target):
        return pltpu.make_async_remote_copy(
            src_ref=src, dst_ref=dst, send_sem=ss, recv_sem=rs,
            device_id=target, device_id_type=MESH,
        )

    def block_rows(i):
        return pl.ds(pl.multiple_of(i * tile, tile), tile)

    def chunk_rows(i):
        return pl.ds(pl.multiple_of(i * CHUNK, CHUNK), CHUNK)

    def chunk_of(h, i):
        return h[pl.ds(i * per_chunk, per_chunk)].reshape(CHUNK, width)

    def all_of(h):
        return h[...].reshape(rows, width)

    def lent_block(d, i):
        return lists_ref[(sec * 2 + d) * lent + i]

    def send_messages(layer, h):
        copies = []
        for d, target in ((0, upper), (1, lower)):
            for i in range(lent):
                rows_i = h[lent_block(d, i)]
                lend[layer, d, i * tile : (i + 1) * tile, :] = mm(rows_i, wm_ref[layer]).astype(BF)
            c = remote(
                lend.at[layer, d], halo.at[layer, d],
                halo_ss.at[layer, d], halo_rs.at[layer, d], (dp, target),
            )
            c.start()
            copies.append(c)
        return copies

    def own_messages(layer, h):
        @pl.loop(0, chunks)
        def _(i):
            msg[chunk_rows(i), :] = mm(chunk_of(h, i), wm_ref[layer]).astype(BF)

    def own_pre(layer, h, pre):
        @pl.loop(0, chunks)
        def _(i):
            r = chunk_rows(i)
            pre[r, :] = mm(a_own[r, :], msg[...]) + mm(chunk_of(h, i), ws_ref[layer])

    half = lent * tile

    def halo_part(layer, r):
        return mm(a_halo[r, :half], halo[layer, 0]) + mm(a_halo[r, half:], halo[layer, 1])

    def put_dpre(r, i, d):
        dpre[r, :] = d
        for j in range(per_chunk):
            at = pl.ds(pl.multiple_of(i * CHUNK + j * tile, tile), tile)
            dpre_t[:, at] = d[j * tile : (j + 1) * tile, :].T

    loads[0].wait()
    pl.semaphore_wait(barrier, nsec - 1 + ndp - 1)

    sends = send_messages(0, h0)
    own_messages(0, h0)
    loads[1].wait()

    slots = blocks + 2 * lent
    strip = 32

    @pl.loop(0, blocks)
    def _(b):
        for s in range(slots):
            on = [
                jnp.full((16, tile), pick_ref[(b * listed + k) * slots + s], F32).astype(BF)
                for k in range(listed)
            ]
            for j in range(tile // strip):
                cut = slice(j * strip, (j + 1) * strip)
                acc = [
                    tiles[b * listed + k, cut, :] * jnp.concatenate([on[k]] * (strip // 16), axis=0)
                    for k in range(listed)
                ]
                while len(acc) > 1:
                    acc = [x + y for x, y in zip(acc[::2], acc[1::2])]
                at = pl.ds(pl.multiple_of(b * tile + j * strip, strip), strip)
                if s < blocks:
                    a_own[at, s * tile : (s + 1) * tile] = acc[0]
                else:
                    o = s - blocks
                    a_halo[at, o * tile : (o + 1) * tile] = acc[0]

    own_pre(0, h0, pre0)
    for c in sends:
        c.wait()

    @pl.loop(0, chunks)
    def _(i):
        r = chunk_rows(i)
        pre = pre0[r, :] + halo_part(0, r)
        pre0[r, :] = pre
        out = (chunk_of(h0, i).astype(F32) + pre * jax.nn.sigmoid(pre)).astype(BF)
        h1[pl.ds(i * per_chunk, per_chunk)] = out.reshape(per_chunk, tile, width)

    sends = send_messages(1, h1)
    own_messages(1, h1)
    own_pre(1, h1, pre1)

    @pl.loop(0, chunks)
    def _(i):
        r = chunk_rows(i)
        pre0[r, :] = silu_grad(pre0[r, :])

    loads[2].wait()
    for c in sends:
        c.wait()

    @pl.loop(0, chunks)
    def _(i):
        r = chunk_rows(i)
        pre = pre1[r, :] + halo_part(1, r)
        sig = jax.nn.sigmoid(pre)
        h2[r, :] = (chunk_of(h1, i).astype(F32) + pre * sig).astype(BF)
        put_dpre(r, i, (g[r, :] * (sig * (1.0 + pre * (1.0 - sig)))).astype(BF))

    hit_store = pltpu.make_async_copy(h2, hit_out, store_sem.at[0])
    hit_store.start()

    def send_back(layer):
        copies = []
        for d, target in ((0, lower), (1, upper)):
            for i in range(lent // 2):
                lo = (d * lent + 2 * i) * tile
                res = mm(dpre_t[...], a_halo[:, lo : lo + 2 * tile]).astype(BF)
                back_send[layer, d, 2 * i] = res[:, :tile]
                back_send[layer, d, 2 * i + 1] = res[:, tile:]
            c = remote(
                back_send.at[layer, d], back_recv[layer].at[d],
                back_ss.at[layer, d], back_rs.at[layer, d], (dp, target),
            )
            c.start()
            copies.append(c)
        return copies

    def put_part(m, step_t):
        step = step_t.T.astype(BF)
        part[m, :width, :] = step[:, :128]
        part[m, width:, :] = step[:, 128:]

    def own_back(layer, h):
        @pl.loop(0, chunks)
        def _(i):
            own_t[:, chunk_rows(i)] = mm(dpre_t[...], a_own[:, chunk_rows(i)])
            r = chunk_rows(i)
            g[r, :] = g[r, :] + mm_bt(dpre[r, :], ws_ref[layer])

    def finish_back(layer):
        @pl.loop(0, chunks)
        def _(i):
            blocks_t = []
            for j in range(per_chunk):
                b = i * per_chunk + j
                at = block_rows(b)
                total = own_t[:, at]
                for d in range(2):
                    pos = back_pos[d * blocks + b]
                    total = total + back_recv[layer][d, pos].astype(F32) * back_on[d * blocks + b]
                total = total.astype(BF)
                dmsg_t[:, at] = total
                blocks_t.append(total.T)
            r = chunk_rows(i)
            new = g[r, :] + mm_bt(jnp.concatenate(blocks_t, axis=0), wm_ref[layer])
            g[r, :] = new
            if layer == 1:
                put_dpre(r, i, (new * pre0[r, :]).astype(BF))

    bounds = ((0, 3), (3, 1))

    def rs1_start(batch):
        m0, nb = bounds[batch]
        copies = []
        for o, p in enumerate(dp_peers):
            at = pl.ds(pl.multiple_of(p * r1, r1), r1)
            c = remote(
                part.at[pl.ds(m0, nb), at], rs1.at[o, pl.ds(m0, nb)],
                rs1_ss.at[batch, o], rs1_rs.at[batch, o], (p, sec),
            )
            c.start()
            copies.append(c)
        return copies

    def rs2_start(batch, copies):
        m0, nb = bounds[batch]
        for c in copies:
            c.wait()
        own = pl.ds(pl.multiple_of(dp * r1, r1), r1)
        for m in range(m0, m0 + nb):
            total = part[m, own, :].astype(F32)
            for o in range(ndp - 1):
                total = total + rs1[o, m].astype(F32)
            q1[m] = total.astype(BF)
        out = []
        for o, p in enumerate(sec_peers):
            piece = lax.rem(p, owners)
            at = pl.ds(pl.multiple_of(piece * r2, r2), r2)
            c = remote(
                q1.at[pl.ds(m0, nb), at], rs2.at[o, pl.ds(m0, nb)],
                rs2_ss.at[batch, o], rs2_rs.at[batch, o], (dp, p),
            )
            cond(p < owners, c.start)
            out.append((p, c))
        return out

    def ag2_start(batch, copies):
        m0, nb = bounds[batch]
        mine = lax.rem(sec, owners)
        at = pl.ds(pl.multiple_of(mine * r2, r2), r2)
        for p, c in copies:
            cond(p < owners, c.wait_send)
            cond(sec < owners, c.wait_recv)

        def total_up():
            for m in range(m0, m0 + nb):
                total = q1[m, at, :].astype(F32)
                for o in range(nsec - 1):
                    total = total + rs2[o, m].astype(F32)
                r_own[m] = total.astype(BF)
                g2[m, at, :] = r_own[m]

        cond(sec < owners, total_up)
        out = []
        for o, p in enumerate(sec_peers):
            c = remote(
                r_own.at[pl.ds(m0, nb)], g2.at[pl.ds(m0, nb), at],
                ag2_ss.at[batch, o], ag2_rs.at[batch, o], (dp, p),
            )
            cond(sec < owners, c.start)
            source = lax.rem(sec + nsec - 1 - o, nsec)
            out.append((source, c))
        return out

    def ag1_start(batch, copies):
        m0, nb = bounds[batch]
        for source, c in copies:
            cond(sec < owners, c.wait_send)
            cond(source < owners, c.wait_recv)
        at = pl.ds(pl.multiple_of(dp * r1, r1), r1)
        for m in range(m0, m0 + nb):
            g1[m, at, :] = g2[m]
        out = []
        for o, p in enumerate(dp_peers):
            c = remote(
                g2.at[pl.ds(m0, nb)], g1.at[pl.ds(m0, nb), at],
                ag1_ss.at[batch, o], ag1_rs.at[batch, o], (p, sec),
            )
            c.start()
            out.append(c)
        return out

    sends = send_back(1)
    put_part(0, mm(dpre_t[...], all_of(h1)))
    own_back(1, h1)
    for c in sends:
        c.wait()
    finish_back(1)

    sends = send_back(0)
    put_part(1, mm(dmsg_t[...], all_of(h1)))
    put_part(2, mm(dpre_t[...], all_of(h0)))
    first = rs1_start(0)
    own_back(0, h0)
    first = rs2_start(0, first)
    first = ag2_start(0, first)
    for c in sends:
        c.wait()
    finish_back(0)
    put_part(3, mm(dmsg_t[...], all_of(h0)))
    second = rs1_start(1)
    grad_store = pltpu.make_async_copy(g, grad_out, store_sem.at[1])
    grad_store.start()
    first = ag1_start(0, first)
    second = rs2_start(1, second)
    second = ag2_start(1, second)
    second = ag1_start(1, second)
    for c in first + second:
        c.wait()
    for m, out, layer in ((0, sg_out, 1), (1, mg_out, 1), (2, sg_out, 0), (3, mg_out, 0)):
        out[layer, :, :128] = g1[m, :width, :].astype(F32)
        out[layer, :, 128:] = g1[m, width:, :].astype(F32)
    hit_store.wait()
    grad_store.wait()


def per_device(ndp, nsec, hits, tiles, sources, send_list, w_message, w_self, cotangent):
    blocks, listed, tile = tiles.shape[1], tiles.shape[2], tiles.shape[3]
    rows, width = hits.shape[1], hits.shape[2]
    lent = send_list.shape[3]
    folded = 2 * width
    r1 = folded // ndp
    r2 = max(16, r1 // nsec)
    slots = jnp.arange(blocks + 2 * lent, dtype=jnp.int32)
    picks = (sources[0][:, :, None] == slots).astype(F32)
    own_lists = lax.dynamic_index_in_dim(send_list[0], lax.axis_index("sector"), 0, keepdims=False)
    match = own_lists[:, None, :] == slots[:blocks, None]
    back_pos = jnp.sum(match * jnp.arange(lent, dtype=jnp.int32), axis=-1).astype(jnp.int32)
    back_on = jnp.any(match, axis=-1).astype(F32)
    vmem, sem = pltpu.VMEM, pltpu.SemaphoreType.DMA
    scratch = [
        vmem((blocks, tile, width), BF), vmem((blocks, tile, width), BF), vmem((rows, width), BF),
        vmem((blocks * listed, tile, tile), BF),
        vmem((rows, width), F32), vmem((rows, width), F32), vmem((rows, width), F32),
        vmem((rows, width), BF),
        vmem((rows, rows), BF), vmem((rows, 2 * lent * tile), BF),
        vmem((LAYERS, 2, lent * tile, width), BF), vmem((LAYERS, 2, lent * tile, width), BF),
        vmem((rows, width), BF), vmem((width, rows), BF), vmem((width, rows), BF),
        vmem((width, rows), F32),
        vmem((LAYERS, 2, lent, width, tile), BF),
        vmem((2, lent, width, tile), BF), vmem((2, lent, width, tile), BF),
        vmem((4, folded, 128), BF), vmem((ndp - 1, 4, r1, 128), BF), vmem((4, r1, 128), BF),
        vmem((nsec - 1, 4, r2, 128), BF), vmem((4, r2, 128), BF), vmem((4, r1, 128), BF),
        vmem((4, folded, 128), BF),
        sem((3,)), sem((2,)), sem((LAYERS, 2)), sem((LAYERS, 2)), sem((LAYERS, 2)), sem((LAYERS, 2)),
        sem((2, ndp - 1)), sem((2, ndp - 1)), sem((2, nsec - 1)), sem((2, nsec - 1)),
        sem((2, nsec - 1)), sem((2, nsec - 1)), sem((2, ndp - 1)), sem((2, ndp - 1)),
    ]
    flat = pl.BlockSpec(memory_space=pltpu.SMEM)
    far = pl.BlockSpec(memory_space=pl.ANY)
    near = pl.BlockSpec(memory_space=pltpu.VMEM)
    hit_output, grad, message_total, self_total = pl.pallas_call(
        functools.partial(kernel, ndp, nsec, blocks, listed, lent, tile, width, r1, r2),
        out_shape=(
            jax.ShapeDtypeStruct((rows, width), BF),
            jax.ShapeDtypeStruct((rows, width), F32),
            jax.ShapeDtypeStruct(w_message.shape, F32),
            jax.ShapeDtypeStruct(w_self.shape, F32),
        ),
        in_specs=[flat, flat, flat, flat, far, far, far, near, near],
        out_specs=(far, far, near, near),
        scratch_shapes=scratch,
        compiler_params=pltpu.CompilerParams(
            collective_id=0, has_side_effects=True, vmem_limit_bytes=56 * 1024 * 1024
        ),
    )(
        picks.reshape(-1), send_list.reshape(-1), back_pos.reshape(-1), back_on.reshape(-1),
        hits[0].reshape(blocks, tile, width),
        tiles.reshape(blocks * listed, tile, tile), cotangent[0], w_message, w_self,
    )
    total_rows = rows * ndp * nsec
    scale = 1.0 / jnp.sqrt(jnp.float32(total_rows))
    return (hit_output[None], grad[None], message_total * scale, self_total * scale)


def solution(mesh):
    in_specs = (
        P("dp", "sector", None),
        P("dp", "sector", None, None, None),
        P("dp", "sector", None),
        P("dp", None, None, None),
        P(),
        P(),
        P("dp", "sector", None),
    )
    out_specs = (P("dp", "sector", None), P("dp", "sector", None), P(), P())
    return jax.shard_map(
        functools.partial(per_device, mesh.shape["dp"], mesh.shape["sector"]),
        mesh=mesh, in_specs=in_specs, out_specs=out_specs, check_vma=False,
    )
```

time: 407 us -> 108 us (0.27); the launches traced: 400 us -> 107 us
  waiting for transfers between devices: 178 us -> 0 us
  Pallas kernels: 0 us -> 96.7 us
  local copies, waits for them, and re-layouts: 77 us -> 7.21 us
  other arithmetic: 61.7 us -> 2.67 us
  matrix products: 50.2 us -> 0 us
  starting transfers between devices: 18 us -> 0 us
  between operations: 14.9 us -> 0.68 us
    psum x1 -> x0, waiting for transfers between devices: 128 us -> none  [per_device(): lax.psum((message_total, self_total), ('dp', 'sector'))]
    pallas_call x0 -> x1, Pallas kernels: none -> 96.7 us  [per_device(): pl.pallas_call(functools.partial(kernel, ndp, nsec, blocks, listed, lent,...]
    scatter-add x6 -> x0, other arithmetic: 58.2 us -> none  [the longest x2 50.7 us: per_device(): jax.ops.segment_sum(contrib.reshape(blocks_here * listed, tile_rows * wid...]
    dot_general x16 -> x0, matrix products: 50.2 us -> none  [the longest x2 16.2 us: per_device(): jnp.einsum('bkij,bif->bkjf', tile_data, dpre.reshape(blocks_here, tile_ro...]
    ppermute x8 -> x0, waiting for transfers between devices: 49.9 us -> none  [the longest x4 37.6 us: extended_2(): lax.ppermute(tail, axis, [(i, (i + 1) % count) for i in range(count)])]
    unnamed x61 -> x7, local copies, waits for them, and re-layouts: 45.9 us -> 3.07 us
    ppermute x8 -> x0, starting transfers between devices: 17.9 us -> none  [the longest x4 15.5 us: extended_2(): lax.ppermute(head, axis, [((i + 1) % count, i) for i in range(count)])]
    gather x6 -> x0, local copies, waits for them, and re-layouts: 15.5 us -> none  [the longest x2 13.2 us: per_device(): gathered = table[slot_ids]]
  transfers between devices with their start and end apart: 9 -> 0, of which waited for: 9 -> 0; matrix products, arithmetic and copies ran while one was open for 4% -> 0% of each run, Pallas kernels for 0% -> 0%
where the time goes in v1:
time: 108 us; the launch traced here: 107 us
  Pallas kernels  96.7 us (90%)
  local copies, waits for them, and re-layouts  7.21 us (7%)
  other arithmetic  2.67 us (2%)
    pallas_call x1, Pallas kernels, per_device(): pl.pallas_call(functools.partial(kernel, ndp, nsec, blocks, listed, lent,...  96.7 us
    unnamed x7, local copies, waits for them, and re-layouts  3.07 us
    mul x1, other arithmetic, per_device(): self_total * scale  2.4 us

profile of v1, /device:TPU:1, one launch (start us, length us, event | category | flops | bytes accessed | tf_op | source)
XLA Modules:
  0.0 107.2 jit_solution(5994451955275663300)
XLA Ops:
  0.6 0.9 dynamic-slice_reduce_fusion
  1.5 0.1 compare_reduce_fusion
  1.6 0.1 fusion.1
  1.7 0.6 reshape.34.back_pos
  2.3 0.6 reshape.37.back_on
  2.9 0.8 copy.15
  3.7 0.8 copy.16
  4.4 0.6 reshape.33.lists_ref
  5.1 0.1 fusion
  5.1 0.7 reshape.36.pick_ref
  5.8 96.7 %shard_map.102 = (bf16[2048,256]{1,0:T(8,128)(2,1)}, f32[2048,256]{1,0:T(8,128)}, f32[2,256,256]{2,1,0:T(8,128)}, f32[2,256,256]{2,1,0:T(8,128)}) custom-call(f32[3072]{0:T(1024)} %reshape.36.pick_ref, s32[64]{0:T(128)} %reshape.33.lists_ref, s32[32]{0:T(128)} %reshape.34.back_pos, f32[32]{0:T(128)} %reshape.37.back_on, bf16[16,128,256]{2,1,0:T(8,128)(2,1)} %bitcast.10, ...), custom_call_target="tpu_custom_call" | custom-call | tf_op jit(solution)/shard_map/pallas_call | solution.py:397
  102.5 0.0 copy-start.1
  102.5 0.0 copy-start
  102.5 2.4 %broadcast_multiply_fusion = (f32[2,256,256]{2,1,0:T(8,128)}, f32[2,256,256]{2,1,0:T(8,128)}) fusion(f32[2,256,256]{2,1,0:T(8,128)} %get-tuple-element.11, f32[2,256,256]{2,1,0:T(8,128)} %get-tuple-element.10), kind=kLoop, calls=%fused_computation | loop fusion | flops 262144 | bytes 2097152 | tf_op jit(solution)/shard_map/mul | solution.py:418
  104.9 0.0 copy-done.1
  104.9 1.0 copy.19
  105.9 0.0 copy-done
  105.9 1.3 %copy.20 = f32[1,2048,256]{2,1,0:T(8,128)} copy(f32[1,2048,256]{2,1,0:T(8,128)S(1)} %bitcast.9) | data formatting | bytes 4194304
  (2 shorter events, 0.0 us)
Async XLA Ops:
  102.5 2.4 %copy-start.1 = (bf16[2048,256]{1,0:T(8,128)(2,1)S(1)}, bf16[2048,256]{1,0:T(8,128)(2,1)}, u32[]{:S(2)}) copy-start(bf16[2048,256]{1,0:T(8,128)(2,1)} %get-tuple-element.8) | copy-start | bytes 3145732
  102.5 3.4 %copy-start = (f32[2048,256]{1,0:T(8,128)S(1)}, f32[2048,256]{1,0:T(8,128)}, u32[]{:S(2)}) copy-start(f32[2048,256]{1,0:T(8,128)} %get-tuple-element.9) | copy-start | bytes 6291460

commit v2 on v1

--- a/solution.py
+++ b/solution.py
@@ -29,9 +29,9 @@
 
 def kernel(
     ndp, nsec, blocks, listed, lent, tile, width, r1, r2,
-    pick_ref, lists_ref, back_pos, back_on, hits_hbm, tiles_hbm, cot_hbm, wm_ref, ws_ref,
+    table, hits_hbm, tiles_hbm, cot_hbm, wm_hbm, ws_hbm,
     hit_out, grad_out, mg_out, sg_out,
-    h0, h1, h2, tiles, g, pre0, pre1, msg, a_own, a_halo, halo, lend,
+    h0, h1, h2, tiles, g, wm_ref, ws_ref, pre0, pre1, msg, hmsg, a_own, a_halo, halo, lend,
     dpre, dpre_t, dmsg_t, own_t, back_send, back_recv0, back_recv1,
     part, rs1, q1, rs2, r_own, g2, g1,
     load_sem, store_sem, halo_ss, halo_rs, back_ss, back_rs,
@@ -51,8 +51,10 @@
 
     loads = [
         pltpu.make_async_copy(hits_hbm, h0, load_sem.at[0]),
-        pltpu.make_async_copy(tiles_hbm, tiles, load_sem.at[1]),
-        pltpu.make_async_copy(cot_hbm, g, load_sem.at[2]),
+        pltpu.make_async_copy(wm_hbm, wm_ref, load_sem.at[1]),
+        pltpu.make_async_copy(tiles_hbm, tiles.at[pl.ds(0, blocks * listed)], load_sem.at[2]),
+        pltpu.make_async_copy(ws_hbm, ws_ref, load_sem.at[3]),
+        pltpu.make_async_copy(cot_hbm, g, load_sem.at[4]),
     ]
     for c in loads:
         c.start()
@@ -88,14 +90,12 @@
         return h[...].reshape(rows, width)
 
     def lent_block(d, i):
-        return lists_ref[(sec * 2 + d) * lent + i]
-
-    def send_messages(layer, h):
+        return table[d * lent + i]
+
+    def send_lent(layer, make):
         copies = []
         for d, target in ((0, upper), (1, lower)):
-            for i in range(lent):
-                rows_i = h[lent_block(d, i)]
-                lend[layer, d, i * tile : (i + 1) * tile, :] = mm(rows_i, wm_ref[layer]).astype(BF)
+            lend[layer, d] = make([lent_block(d, i) for i in range(lent)])
             c = remote(
                 lend.at[layer, d], halo.at[layer, d],
                 halo_ss.at[layer, d], halo_rs.at[layer, d], (dp, target),
@@ -113,12 +113,18 @@
         @pl.loop(0, chunks)
         def _(i):
             r = chunk_rows(i)
-            pre[r, :] = mm(a_own[r, :], msg[...]) + mm(chunk_of(h, i), ws_ref[layer])
+            out = mm(a_own[r, :], msg[...]) + mm(chunk_of(h, i), ws_ref[layer])
+            pre[pl.ds(i * per_chunk, per_chunk)] = out.reshape(per_chunk, tile, width)
 
     half = lent * tile
 
-    def halo_part(layer, r):
-        return mm(a_halo[r, :half], halo[layer, 0]) + mm(a_halo[r, half:], halo[layer, 1])
+    def halo_messages(layer):
+        for d in range(2):
+            hmsg[d * half : (d + 1) * half, :] = mm(halo[layer, d], wm_ref[layer]).astype(BF)
+
+    def halo_part(i):
+        rows_a = a_halo[pl.ds(i * per_chunk, per_chunk)].reshape(CHUNK, 2 * half)
+        return mm(rows_a, hmsg[...])
 
     def put_dpre(r, i, d):
         dpre[r, :] = d
@@ -129,64 +135,65 @@
     loads[0].wait()
     pl.semaphore_wait(barrier, nsec - 1 + ndp - 1)
 
-    sends = send_messages(0, h0)
+    sends = send_lent(0, lambda ids: jnp.concatenate([h0[b] for b in ids], axis=0))
+    loads[1].wait()
     own_messages(0, h0)
-    loads[1].wait()
+    tiles[blocks * listed] = jnp.zeros((tile, tile), BF)
+    back_recv0[:, lent] = jnp.zeros((2, width, tile), BF)
+    back_recv1[:, lent] = jnp.zeros((2, width, tile), BF)
+    loads[2].wait()
 
     slots = blocks + 2 * lent
-    strip = 32
+    at_first = 2 * lent + 2 * blocks
+    at_next = at_first + blocks * slots
 
     @pl.loop(0, blocks)
     def _(b):
+        for k in reversed(range(listed - 1)):
+            e = b * listed + k
+            tiles[e] = tiles[e] + tiles[table[at_next + e]]
         for s in range(slots):
-            on = [
-                jnp.full((16, tile), pick_ref[(b * listed + k) * slots + s], F32).astype(BF)
-                for k in range(listed)
-            ]
-            for j in range(tile // strip):
-                cut = slice(j * strip, (j + 1) * strip)
-                acc = [
-                    tiles[b * listed + k, cut, :] * jnp.concatenate([on[k]] * (strip // 16), axis=0)
-                    for k in range(listed)
-                ]
-                while len(acc) > 1:
-                    acc = [x + y for x, y in zip(acc[::2], acc[1::2])]
-                at = pl.ds(pl.multiple_of(b * tile + j * strip, strip), strip)
-                if s < blocks:
-                    a_own[at, s * tile : (s + 1) * tile] = acc[0]
-                else:
-                    o = s - blocks
-                    a_halo[at, o * tile : (o + 1) * tile] = acc[0]
-
+            val = tiles[table[at_first + b * slots + s]]
+            if s < blocks:
+                a_own[block_rows(b), s * tile : (s + 1) * tile] = val
+            else:
+                o = s - blocks
+                a_halo[b, :, o * tile : (o + 1) * tile] = val
+
+    loads[3].wait()
     own_pre(0, h0, pre0)
     for c in sends:
         c.wait()
+    halo_messages(0)
+
+    def layer_out(h, pre):
+        return (h.astype(F32) + pre * jax.nn.sigmoid(pre)).astype(BF)
+
+    def lent_out(ids):
+        pre = jnp.concatenate([pre0[b] for b in ids], axis=0)
+        pre = pre + mm(jnp.concatenate([a_halo[b] for b in ids], axis=0), hmsg[...])
+        return layer_out(jnp.concatenate([h0[b] for b in ids], axis=0), pre)
+
+    sends = send_lent(1, lent_out)
+
+    @pl.loop(0, chunks)
+    def _(i):
+        at = pl.ds(i * per_chunk, per_chunk)
+        pre = chunk_of(pre0, i) + halo_part(i)
+        h1[at] = layer_out(chunk_of(h0, i), pre).reshape(per_chunk, tile, width)
+        pre0[at] = silu_grad(pre).reshape(per_chunk, tile, width)
+
+    own_messages(1, h1)
+    own_pre(1, h1, pre1)
+    loads[4].wait()
+    for c in sends:
+        c.wait()
+    halo_messages(1)
 
     @pl.loop(0, chunks)
     def _(i):
         r = chunk_rows(i)
-        pre = pre0[r, :] + halo_part(0, r)
-        pre0[r, :] = pre
-        out = (chunk_of(h0, i).astype(F32) + pre * jax.nn.sigmoid(pre)).astype(BF)
-        h1[pl.ds(i * per_chunk, per_chunk)] = out.reshape(per_chunk, tile, width)
-
-    sends = send_messages(1, h1)
-    own_messages(1, h1)
-    own_pre(1, h1, pre1)
-
-    @pl.loop(0, chunks)
-    def _(i):
-        r = chunk_rows(i)
-        pre0[r, :] = silu_grad(pre0[r, :])
-
-    loads[2].wait()
-    for c in sends:
-        c.wait()
-
-    @pl.loop(0, chunks)
-    def _(i):
-        r = chunk_rows(i)
-        pre = pre1[r, :] + halo_part(1, r)
+        pre = chunk_of(pre1, i) + halo_part(i)
         sig = jax.nn.sigmoid(pre)
         h2[r, :] = (chunk_of(h1, i).astype(F32) + pre * sig).astype(BF)
         put_dpre(r, i, (g[r, :] * (sig * (1.0 + pre * (1.0 - sig)))).astype(BF))
@@ -199,15 +206,16 @@
         for d, target in ((0, lower), (1, upper)):
             for i in range(lent // 2):
                 lo = (d * lent + 2 * i) * tile
-                res = mm(dpre_t[...], a_halo[:, lo : lo + 2 * tile]).astype(BF)
+                a_cols = a_halo[:, :, lo : lo + 2 * tile].reshape(rows, 2 * tile)
+                res = mm(dpre_t[...], a_cols).astype(BF)
                 back_send[layer, d, 2 * i] = res[:, :tile]
                 back_send[layer, d, 2 * i + 1] = res[:, tile:]
-            c = remote(
-                back_send.at[layer, d], back_recv[layer].at[d],
-                back_ss.at[layer, d], back_rs.at[layer, d], (dp, target),
-            )
-            c.start()
-            copies.append(c)
+                c = remote(
+                    back_send.at[layer, d, pl.ds(2 * i, 2)], back_recv[layer].at[d, pl.ds(2 * i, 2)],
+                    back_ss.at[layer, d, i], back_rs.at[layer, d, i], (dp, target),
+                )
+                c.start()
+                copies.append(c)
         return copies
 
     def put_part(m, step_t):
@@ -218,9 +226,18 @@
     def own_back(layer, h):
         @pl.loop(0, chunks)
         def _(i):
-            own_t[:, chunk_rows(i)] = mm(dpre_t[...], a_own[:, chunk_rows(i)])
+            out = mm(dpre_t[...], a_own[:, chunk_rows(i)])
+            own_t[:, chunk_rows(i)] = out
+            dmsg_t[:, chunk_rows(i)] = out.astype(BF)
             r = chunk_rows(i)
             g[r, :] = g[r, :] + mm_bt(dpre[r, :], ws_ref[layer])
+
+    def message_part(layer, h):
+        total = mm(dmsg_t[...], all_of(h))
+        for d in range(2):
+            for i in range(lent):
+                total = total + mm(back_send[layer, d, i], halo[layer, d, i * tile : (i + 1) * tile, :])
+        return total
 
     def finish_back(layer):
         @pl.loop(0, chunks)
@@ -231,18 +248,17 @@
                 at = block_rows(b)
                 total = own_t[:, at]
                 for d in range(2):
-                    pos = back_pos[d * blocks + b]
-                    total = total + back_recv[layer][d, pos].astype(F32) * back_on[d * blocks + b]
+                    pos = table[2 * lent + d * blocks + b]
+                    total = total + back_recv[layer][d, pos].astype(F32)
                 total = total.astype(BF)
-                dmsg_t[:, at] = total
                 blocks_t.append(total.T)
             r = chunk_rows(i)
             new = g[r, :] + mm_bt(jnp.concatenate(blocks_t, axis=0), wm_ref[layer])
             g[r, :] = new
             if layer == 1:
-                put_dpre(r, i, (new * pre0[r, :]).astype(BF))
-
-    bounds = ((0, 3), (3, 1))
+                put_dpre(r, i, (new * chunk_of(pre0, i)).astype(BF))
+
+    bounds = ((0, 2), (2, 2))
 
     def rs1_start(batch):
         m0, nb = bounds[batch]
@@ -328,33 +344,34 @@
     sends = send_back(1)
     put_part(0, mm(dpre_t[...], all_of(h1)))
     own_back(1, h1)
-    for c in sends:
-        c.wait()
-    finish_back(1)
-
-    sends = send_back(0)
-    put_part(1, mm(dmsg_t[...], all_of(h1)))
-    put_part(2, mm(dpre_t[...], all_of(h0)))
+    put_part(1, message_part(1, h1))
     first = rs1_start(0)
-    own_back(0, h0)
     first = rs2_start(0, first)
     first = ag2_start(0, first)
     for c in sends:
         c.wait()
-    finish_back(0)
-    put_part(3, mm(dmsg_t[...], all_of(h0)))
+    finish_back(1)
+
+    sends = send_back(0)
+    put_part(2, mm(dpre_t[...], all_of(h0)))
+    own_back(0, h0)
+    put_part(3, message_part(0, h0))
     second = rs1_start(1)
-    grad_store = pltpu.make_async_copy(g, grad_out, store_sem.at[1])
-    grad_store.start()
     first = ag1_start(0, first)
     second = rs2_start(1, second)
     second = ag2_start(1, second)
+    for c in sends:
+        c.wait()
+    finish_back(0)
+    grad_store = pltpu.make_async_copy(g, grad_out, store_sem.at[1])
+    grad_store.start()
     second = ag1_start(1, second)
     for c in first + second:
         c.wait()
+    scale = 1.0 / (float(rows * ndp * nsec) ** 0.5)
     for m, out, layer in ((0, sg_out, 1), (1, mg_out, 1), (2, sg_out, 0), (3, mg_out, 0)):
-        out[layer, :, :128] = g1[m, :width, :].astype(F32)
-        out[layer, :, 128:] = g1[m, width:, :].astype(F32)
+        out[layer, :, :128] = g1[m, :width, :].astype(F32) * scale
+        out[layer, :, 128:] = g1[m, width:, :].astype(F32) * scale
     hit_store.wait()
     grad_store.wait()
 
@@ -366,28 +383,41 @@
     folded = 2 * width
     r1 = folded // ndp
     r2 = max(16, r1 // nsec)
-    slots = jnp.arange(blocks + 2 * lent, dtype=jnp.int32)
-    picks = (sources[0][:, :, None] == slots).astype(F32)
     own_lists = lax.dynamic_index_in_dim(send_list[0], lax.axis_index("sector"), 0, keepdims=False)
-    match = own_lists[:, None, :] == slots[:blocks, None]
-    back_pos = jnp.sum(match * jnp.arange(lent, dtype=jnp.int32), axis=-1).astype(jnp.int32)
-    back_on = jnp.any(match, axis=-1).astype(F32)
+    places = jnp.arange(blocks + 2 * lent, dtype=jnp.int32)
+    turn = jnp.arange(lent, dtype=jnp.int32)
+    match = own_lists[:, None, :] == places[:blocks, None]
+    back_pos = jnp.min(jnp.where(match, turn, lent), axis=-1)
+    ids = sources[0]
+    order = jnp.arange(listed, dtype=jnp.int32)
+    entry = jnp.arange(blocks, dtype=jnp.int32)[:, None] * listed
+    none = blocks * listed
+    first = jnp.min(
+        jnp.where(ids[:, None, :] == places[:, None], entry[:, :, None] + order, none), axis=-1
+    )
+    later = (ids[:, None, :] == ids[:, :, None]) & (order > order[:, None])
+    following = jnp.min(jnp.where(later, entry[:, :, None] + order, none), axis=-1)
+    table = jnp.concatenate(
+        [own_lists.reshape(-1), back_pos.reshape(-1), first.reshape(-1), following.reshape(-1)]
+    ).astype(jnp.int32)
     vmem, sem = pltpu.VMEM, pltpu.SemaphoreType.DMA
     scratch = [
         vmem((blocks, tile, width), BF), vmem((blocks, tile, width), BF), vmem((rows, width), BF),
-        vmem((blocks * listed, tile, tile), BF),
-        vmem((rows, width), F32), vmem((rows, width), F32), vmem((rows, width), F32),
-        vmem((rows, width), BF),
-        vmem((rows, rows), BF), vmem((rows, 2 * lent * tile), BF),
+        vmem((blocks * listed + 1, tile, tile), BF), vmem((rows, width), F32),
+        vmem(w_message.shape, BF), vmem(w_self.shape, BF),
+        vmem((blocks, tile, width), F32), vmem((blocks, tile, width), F32),
+        vmem((rows, width), BF), vmem((2 * lent * tile, width), BF),
+        vmem((rows, rows), BF), vmem((blocks, tile, 2 * lent * tile), BF),
         vmem((LAYERS, 2, lent * tile, width), BF), vmem((LAYERS, 2, lent * tile, width), BF),
         vmem((rows, width), BF), vmem((width, rows), BF), vmem((width, rows), BF),
         vmem((width, rows), F32),
         vmem((LAYERS, 2, lent, width, tile), BF),
-        vmem((2, lent, width, tile), BF), vmem((2, lent, width, tile), BF),
+        vmem((2, lent + 1, width, tile), BF), vmem((2, lent + 1, width, tile), BF),
         vmem((4, folded, 128), BF), vmem((ndp - 1, 4, r1, 128), BF), vmem((4, r1, 128), BF),
         vmem((nsec - 1, 4, r2, 128), BF), vmem((4, r2, 128), BF), vmem((4, r1, 128), BF),
         vmem((4, folded, 128), BF),
-        sem((3,)), sem((2,)), sem((LAYERS, 2)), sem((LAYERS, 2)), sem((LAYERS, 2)), sem((LAYERS, 2)),
+        sem((5,)), sem((2,)), sem((LAYERS, 2)), sem((LAYERS, 2)),
+        sem((LAYERS, 2, lent // 2)), sem((LAYERS, 2, lent // 2)),
         sem((2, ndp - 1)), sem((2, ndp - 1)), sem((2, nsec - 1)), sem((2, nsec - 1)),
         sem((2, nsec - 1)), sem((2, nsec - 1)), sem((2, ndp - 1)), sem((2, ndp - 1)),
     ]
@@ -402,20 +432,17 @@
             jax.ShapeDtypeStruct(w_message.shape, F32),
             jax.ShapeDtypeStruct(w_self.shape, F32),
         ),
-        in_specs=[flat, flat, flat, flat, far, far, far, near, near],
+        in_specs=[flat, far, far, far, far, far],
         out_specs=(far, far, near, near),
         scratch_shapes=scratch,
         compiler_params=pltpu.CompilerParams(
             collective_id=0, has_side_effects=True, vmem_limit_bytes=56 * 1024 * 1024
         ),
     )(
-        picks.reshape(-1), send_list.reshape(-1), back_pos.reshape(-1), back_on.reshape(-1),
-        hits[0].reshape(blocks, tile, width),
+        table, hits[0].reshape(blocks, tile, width),
         tiles.reshape(blocks * listed, tile, tile), cotangent[0], w_message, w_self,
     )
-    total_rows = rows * ndp * nsec
-    scale = 1.0 / jnp.sqrt(jnp.float32(total_rows))
-    return (hit_output[None], grad[None], message_total * scale, self_total * scale)
+    return (hit_output[None], grad[None], message_total, self_total)
 
 
 def solution(mesh):

time: 108 us -> 92.4 us (0.86)
  Pallas kernels: 96.7 us -> 82.2 us
    pallas_call x1, Pallas kernels: 96.7 us -> 82.2 us  [per_device(): pl.pallas_call(functools.partial(kernel, ndp, nsec, blocks, listed, lent,...]
    unnamed x7 -> x12, local copies, waits for them, and re-layouts: 3.07 us -> 6.06 us
    mul x1, other arithmetic: 2.4 us -> 0.01 us  [per_device(): entry = jnp.arange(blocks, dtype=jnp.int32)[:, None] * listed]
    convert_element_type x2 -> x0, local copies, waits for them, and re-layouts: 1.28 us -> none  [the longest x1 0.69 us: per_device(): picks = (sources[0][:, :, None] == slots).astype(F32)]
where the time goes in v2:
time: 92.4 us; the launch traced here: 92.1 us
  Pallas kernels  82.2 us (89%)
  local copies, waits for them, and re-layouts  7.51 us (8%)
  other arithmetic  1.76 us (2%)
    pallas_call x1, Pallas kernels, per_device(): pl.pallas_call(functools.partial(kernel, ndp, nsec, blocks, listed, lent,...  82.2 us
    unnamed x12, local copies, waits for them, and re-layouts  6.06 us

profile of v2, /device:TPU:1, one launch (start us, length us, event | category | flops | bytes accessed | tf_op | source)
XLA Modules:
  0.0 92.1 jit_solution(15200612441923700812)
XLA Ops:
  0.6 0.0 copy-start
  0.6 0.7 copy-done
  1.3 0.2 dynamic-slice_reduce_fusion
  1.5 0.1 reshape.71
  1.6 0.1 select_reduce_fusion.2
  1.7 0.1 reshape.72
  1.8 0.9 select_reduce_fusion.1
  2.7 0.1 copy.18
  2.8 0.1 copy.19
  2.8 0.1 reshape.74
  2.9 0.8 copy.17
  3.7 0.1 select_reduce_fusion
  3.8 0.1 reshape.73
  3.9 0.7 pad_add_fusion.table
  4.6 82.2 %shard_map.102 = (bf16[2048,256]{1,0:T(8,128)(2,1)}, f32[2048,256]{1,0:T(8,128)}, f32[2,256,256]{2,1,0:T(8,128)}, f32[2,256,256]{2,1,0:T(8,128)}) custom-call(s32[552]{0:T(1024)} %pad_add_fusion.table, bf16[16,128,256]{2,1,0:T(8,128)(2,1)} %bitcast.10, bf16[128,128,128]{2,1,0:T(8,128)(2,1)} %bitcast.7, f32[2048,256]{1,0:T(8,128)} %bitcast.8, ...), custom_call_target="tpu_custom_call" | custom-call | tf_op jit(solution)/shard_map/pallas_call | solution.py:427
  86.7 0.0 copy-start.1
  86.7 2.4 %copy.24 = bf16[1,2048,256]{2,1,0:T(8,128)(2,1)} copy(bf16[1,2048,256]{2,1,0:T(8,128)(2,1)} %bitcast.11) | data formatting | bytes 2097152
  89.1 0.0 copy-done.1
  89.1 0.0 copy-start.3
  89.1 0.0 copy-start.2
  89.2 1.3 %copy.25 = f32[1,2048,256]{2,1,0:T(8,128)} copy(f32[1,2048,256]{2,1,0:T(8,128)S(1)} %bitcast.9) | data formatting | bytes 4194304
  90.5 0.1 copy-done.3
  90.5 0.8 copy.26
  91.3 0.0 copy-done.2
  91.3 0.8 copy.27
  (4 shorter events, 0.0 us)
Async XLA Ops:
  0.6 0.7 copy-start
  86.7 2.4 %copy-start.1 = (f32[2048,256]{1,0:T(8,128)S(1)}, f32[2048,256]{1,0:T(8,128)}, u32[]{:S(2)}) copy-start(f32[2048,256]{1,0:T(8,128)} %get-tuple-element.9) | copy-start | bytes 6291460
  89.1 1.4 %copy-start.3 = (f32[2,256,256]{2,1,0:T(8,128)S(1)}, f32[2,256,256]{2,1,0:T(8,128)}, u32[]{:S(2)}) copy-start(f32[2,256,256]{2,1,0:T(8,128)} %get-tuple-element.18) | copy-start | bytes 1572868
  89.1 2.2 %copy-start.2 = (f32[2,256,256]{2,1,0:T(8,128)S(1)}, f32[2,256,256]{2,1,0:T(8,128)}, u32[]{:S(2)}) copy-start(f32[2,256,256]{2,1,0:T(8,128)} %get-tuple-element.19) | copy-start | bytes 1572868

commit v3 on v2

--- a/solution.py
+++ b/solution.py
@@ -18,10 +18,6 @@
     return lax.dot_general(a, b, (((1,), (0,)), ((), ())), preferred_element_type=F32)
 
 
-def mm_bt(a, b):
-    return lax.dot_general(a, b, (((1,), (1,)), ((), ())), preferred_element_type=F32)
-
-
 def silu_grad(pre):
     sig = jax.nn.sigmoid(pre)
     return sig * (1.0 + pre * (1.0 - sig))
@@ -29,10 +25,10 @@
 
 def kernel(
     ndp, nsec, blocks, listed, lent, tile, width, r1, r2,
-    table, hits_hbm, tiles_hbm, cot_hbm, wm_hbm, ws_hbm,
+    src_ref, lists_ref, hits_hbm, tiles_hbm, cot_hbm, wm_hbm, ws_hbm,
     hit_out, grad_out, mg_out, sg_out,
     h0, h1, h2, tiles, g, wm_ref, ws_ref, pre0, pre1, msg, hmsg, a_own, a_halo, halo, lend,
-    dpre, dpre_t, dmsg_t, own_t, back_send, back_recv0, back_recv1,
+    g_t, sg_t, dpre_t, dmsg_t, own_t, back_send, back_recv0, back_recv1,
     part, rs1, q1, rs2, r_own, g2, g1,
     load_sem, store_sem, halo_ss, halo_rs, back_ss, back_rs,
     rs1_ss, rs1_rs, rs2_ss, rs2_rs, ag2_ss, ag2_rs, ag1_ss, ag1_rs,
@@ -90,12 +86,13 @@
         return h[...].reshape(rows, width)
 
     def lent_block(d, i):
-        return table[d * lent + i]
+        return lists_ref[sec, d, i]
 
     def send_lent(layer, make):
         copies = []
         for d, target in ((0, upper), (1, lower)):
-            lend[layer, d] = make([lent_block(d, i) for i in range(lent)])
+            if make is not None:
+                lend[layer, d] = make([lent_block(d, i) for i in range(lent)])
             c = remote(
                 lend.at[layer, d], halo.at[layer, d],
                 halo_ss.at[layer, d], halo_rs.at[layer, d], (dp, target),
@@ -126,16 +123,17 @@
         rows_a = a_halo[pl.ds(i * per_chunk, per_chunk)].reshape(CHUNK, 2 * half)
         return mm(rows_a, hmsg[...])
 
-    def put_dpre(r, i, d):
-        dpre[r, :] = d
+    def put_turned(dst, i, d):
         for j in range(per_chunk):
             at = pl.ds(pl.multiple_of(i * CHUNK + j * tile, tile), tile)
-            dpre_t[:, at] = d[j * tile : (j + 1) * tile, :].T
+            dst[:, at] = d[j * tile : (j + 1) * tile, :].T
 
     loads[0].wait()
+    for d in range(2):
+        lend[0, d] = jnp.concatenate([h0[lent_block(d, i)] for i in range(lent)], axis=0)
     pl.semaphore_wait(barrier, nsec - 1 + ndp - 1)
 
-    sends = send_lent(0, lambda ids: jnp.concatenate([h0[b] for b in ids], axis=0))
+    sends = send_lent(0, None)
     loads[1].wait()
     own_messages(0, h0)
     tiles[blocks * listed] = jnp.zeros((tile, tile), BF)
@@ -144,16 +142,23 @@
     loads[2].wait()
 
     slots = blocks + 2 * lent
-    at_first = 2 * lent + 2 * blocks
-    at_next = at_first + blocks * slots
+    none = blocks * listed
+
+    def least(pairs):
+        best = jnp.int32(none)
+        for index, away in pairs:
+            best = jnp.minimum(best, index + none * (away * away))
+        return best
 
     @pl.loop(0, blocks)
     def _(b):
+        base = b * listed
+        ids = [src_ref[b, k] for k in range(listed)]
         for k in reversed(range(listed - 1)):
-            e = b * listed + k
-            tiles[e] = tiles[e] + tiles[table[at_next + e]]
+            later = least([(base + m, ids[m] - ids[k]) for m in range(k + 1, listed)])
+            tiles[base + k] = tiles[base + k] + tiles[later]
         for s in range(slots):
-            val = tiles[table[at_first + b * slots + s]]
+            val = tiles[least([(base + k, ids[k] - s) for k in range(listed)])]
             if s < blocks:
                 a_own[block_rows(b), s * tile : (s + 1) * tile] = val
             else:
@@ -181,22 +186,27 @@
         at = pl.ds(i * per_chunk, per_chunk)
         pre = chunk_of(pre0, i) + halo_part(i)
         h1[at] = layer_out(chunk_of(h0, i), pre).reshape(per_chunk, tile, width)
-        pre0[at] = silu_grad(pre).reshape(per_chunk, tile, width)
+        put_turned(sg_t, i, silu_grad(pre))
 
     own_messages(1, h1)
     own_pre(1, h1, pre1)
     loads[4].wait()
+
+    @pl.loop(0, chunks)
+    def _(i):
+        put_turned(g_t, i, g[chunk_rows(i), :])
+
     for c in sends:
         c.wait()
     halo_messages(1)
 
-    @pl.loop(0, chunks)
+    @pl.loop(0, chunks, unroll=2)
     def _(i):
         r = chunk_rows(i)
         pre = chunk_of(pre1, i) + halo_part(i)
         sig = jax.nn.sigmoid(pre)
         h2[r, :] = (chunk_of(h1, i).astype(F32) + pre * sig).astype(BF)
-        put_dpre(r, i, (g[r, :] * (sig * (1.0 + pre * (1.0 - sig)))).astype(BF))
+        put_turned(dpre_t, i, (g[r, :] * (sig * (1.0 + pre * (1.0 - sig)))).astype(BF))
 
     hit_store = pltpu.make_async_copy(h2, hit_out, store_sem.at[0])
     hit_store.start()
@@ -229,8 +239,8 @@
             out = mm(dpre_t[...], a_own[:, chunk_rows(i)])
             own_t[:, chunk_rows(i)] = out
             dmsg_t[:, chunk_rows(i)] = out.astype(BF)
-            r = chunk_rows(i)
-            g[r, :] = g[r, :] + mm_bt(dpre[r, :], ws_ref[layer])
+            c = chunk_rows(i)
+            g_t[:, c] = g_t[:, c] + mm(ws_ref[layer], dpre_t[:, c])
 
     def message_part(layer, h):
         total = mm(dmsg_t[...], all_of(h))
@@ -239,24 +249,28 @@
                 total = total + mm(back_send[layer, d, i], halo[layer, d, i * tile : (i + 1) * tile, :])
         return total
 
-    def finish_back(layer):
-        @pl.loop(0, chunks)
+    def finish_back(layer, lo, hi):
+        @pl.loop(lo, hi, unroll=2)
         def _(i):
-            blocks_t = []
+            c = chunk_rows(i)
+            lent_sum = []
             for j in range(per_chunk):
                 b = i * per_chunk + j
-                at = block_rows(b)
-                total = own_t[:, at]
+                total = jnp.zeros((width, tile), F32)
                 for d in range(2):
-                    pos = table[2 * lent + d * blocks + b]
+                    pos = jnp.int32(lent)
+                    for k in range(lent):
+                        away = lent_block(d, k) - b
+                        pos = jnp.minimum(pos, k + lent * (away * away))
                     total = total + back_recv[layer][d, pos].astype(F32)
-                total = total.astype(BF)
-                blocks_t.append(total.T)
-            r = chunk_rows(i)
-            new = g[r, :] + mm_bt(jnp.concatenate(blocks_t, axis=0), wm_ref[layer])
-            g[r, :] = new
-            if layer == 1:
-                put_dpre(r, i, (new * chunk_of(pre0, i)).astype(BF))
+                lent_sum.append(total)
+            total = (own_t[:, c] + jnp.concatenate(lent_sum, axis=1)).astype(BF)
+            new = g_t[:, c] + mm(wm_ref[layer], total)
+            if layer > 0:
+                g_t[:, c] = new
+                dpre_t[:, c] = (new * sg_t[:, c]).astype(BF)
+            else:
+                g[c, :] = new.T
 
     bounds = ((0, 2), (2, 2))
 
@@ -350,7 +364,7 @@
     first = ag2_start(0, first)
     for c in sends:
         c.wait()
-    finish_back(1)
+    finish_back(1, 0, chunks)
 
     sends = send_back(0)
     put_part(2, mm(dpre_t[...], all_of(h0)))
@@ -362,9 +376,13 @@
     second = ag2_start(1, second)
     for c in sends:
         c.wait()
-    finish_back(0)
-    grad_store = pltpu.make_async_copy(g, grad_out, store_sem.at[1])
-    grad_store.start()
+    grad_stores = []
+    for part_i in range(2):
+        at = pl.ds(part_i * (rows // 2), rows // 2)
+        finish_back(0, part_i * chunks // 2, (part_i + 1) * chunks // 2)
+        c = pltpu.make_async_copy(g.at[at], grad_out.at[at], store_sem.at[1 + part_i])
+        c.start()
+        grad_stores.append(c)
     second = ag1_start(1, second)
     for c in first + second:
         c.wait()
@@ -373,7 +391,21 @@
         out[layer, :, :128] = g1[m, :width, :].astype(F32) * scale
         out[layer, :, 128:] = g1[m, width:, :].astype(F32) * scale
     hit_store.wait()
-    grad_store.wait()
+    for c in grad_stores:
+        c.wait()
+
+
+def finish_kernel(h_in, g_in, m_in, s_in, h_out, g_out, m_out, s_out, sems):
+    copies = []
+    for src, dst, pieces in ((g_in, g_out, 4), (h_in, h_out, 4), (m_in, m_out, 1), (s_in, s_out, 1)):
+        size = src.shape[0] // pieces
+        for p in range(pieces):
+            at = pl.ds(p * size, size)
+            c = pltpu.make_async_copy(src.at[at], dst.at[at], sems.at[len(copies)])
+            c.start()
+            copies.append(c)
+    for c in copies:
+        c.wait()
 
 
 def per_device(ndp, nsec, hits, tiles, sources, send_list, w_message, w_self, cotangent):
@@ -383,23 +415,6 @@
     folded = 2 * width
     r1 = folded // ndp
     r2 = max(16, r1 // nsec)
-    own_lists = lax.dynamic_index_in_dim(send_list[0], lax.axis_index("sector"), 0, keepdims=False)
-    places = jnp.arange(blocks + 2 * lent, dtype=jnp.int32)
-    turn = jnp.arange(lent, dtype=jnp.int32)
-    match = own_lists[:, None, :] == places[:blocks, None]
-    back_pos = jnp.min(jnp.where(match, turn, lent), axis=-1)
-    ids = sources[0]
-    order = jnp.arange(listed, dtype=jnp.int32)
-    entry = jnp.arange(blocks, dtype=jnp.int32)[:, None] * listed
-    none = blocks * listed
-    first = jnp.min(
-        jnp.where(ids[:, None, :] == places[:, None], entry[:, :, None] + order, none), axis=-1
-    )
-    later = (ids[:, None, :] == ids[:, :, None]) & (order > order[:, None])
-    following = jnp.min(jnp.where(later, entry[:, :, None] + order, none), axis=-1)
-    table = jnp.concatenate(
-        [own_lists.reshape(-1), back_pos.reshape(-1), first.reshape(-1), following.reshape(-1)]
-    ).astype(jnp.int32)
     vmem, sem = pltpu.VMEM, pltpu.SemaphoreType.DMA
     scratch = [
         vmem((blocks, tile, width), BF), vmem((blocks, tile, width), BF), vmem((rows, width), BF),
@@ -409,14 +424,14 @@
         vmem((rows, width), BF), vmem((2 * lent * tile, width), BF),
         vmem((rows, rows), BF), vmem((blocks, tile, 2 * lent * tile), BF),
         vmem((LAYERS, 2, lent * tile, width), BF), vmem((LAYERS, 2, lent * tile, width), BF),
-        vmem((rows, width), BF), vmem((width, rows), BF), vmem((width, rows), BF),
-        vmem((width, rows), F32),
+        vmem((width, rows), F32), vmem((width, rows), F32),
+        vmem((width, rows), BF), vmem((width, rows), BF), vmem((width, rows), F32),
         vmem((LAYERS, 2, lent, width, tile), BF),
         vmem((2, lent + 1, width, tile), BF), vmem((2, lent + 1, width, tile), BF),
         vmem((4, folded, 128), BF), vmem((ndp - 1, 4, r1, 128), BF), vmem((4, r1, 128), BF),
         vmem((nsec - 1, 4, r2, 128), BF), vmem((4, r2, 128), BF), vmem((4, r1, 128), BF),
         vmem((4, folded, 128), BF),
-        sem((5,)), sem((2,)), sem((LAYERS, 2)), sem((LAYERS, 2)),
+        sem((5,)), sem((3,)), sem((LAYERS, 2)), sem((LAYERS, 2)),
         sem((LAYERS, 2, lent // 2)), sem((LAYERS, 2, lent // 2)),
         sem((2, ndp - 1)), sem((2, ndp - 1)), sem((2, nsec - 1)), sem((2, nsec - 1)),
         sem((2, nsec - 1)), sem((2, nsec - 1)), sem((2, ndp - 1)), sem((2, ndp - 1)),
@@ -432,16 +447,24 @@
             jax.ShapeDtypeStruct(w_message.shape, F32),
             jax.ShapeDtypeStruct(w_self.shape, F32),
         ),
-        in_specs=[flat, far, far, far, far, far],
+        in_specs=[flat, flat, far, far, far, far, far],
         out_specs=(far, far, near, near),
         scratch_shapes=scratch,
         compiler_params=pltpu.CompilerParams(
             collective_id=0, has_side_effects=True, vmem_limit_bytes=56 * 1024 * 1024
         ),
     )(
-        table, hits[0].reshape(blocks, tile, width),
+        sources[0], send_list[0], hits[0].reshape(blocks, tile, width),
         tiles.reshape(blocks * listed, tile, tile), cotangent[0], w_message, w_self,
     )
+    results = (hit_output, grad, message_total, self_total)
+    hit_output, grad, message_total, self_total = pl.pallas_call(
+        finish_kernel,
+        out_shape=tuple(jax.ShapeDtypeStruct(x.shape, x.dtype) for x in results),
+        in_specs=[far] * 4,
+        out_specs=(far,) * 4,
+        scratch_shapes=[sem((10,))],
+    )(*results)
     return (hit_output[None], grad[None], message_total, self_total)
 
 

time: 92.4 us -> 214 us (2.32)
  Pallas kernels: 82.2 us -> 210 us
  local copies, waits for them, and re-layouts: 7.51 us -> 2.72 us
    pallas_call x0 -> x1, Pallas kernels: none -> 128 us  [per_device(): pl.pallas_call(finish_kernel, out_shape=tuple((jax.ShapeDtypeStruct(x.sha...]
    unnamed x12 -> x0, local copies, waits for them, and re-layouts: 6.06 us -> none
    squeeze x0 -> x2, local copies, waits for them, and re-layouts: none -> 2.72 us  [the longest x1 1.36 us: per_device(): send_list[0]]
where the time goes in v3:
time: 214 us; the launch traced here: 213 us
  Pallas kernels  210 us (98%)
  local copies, waits for them, and re-layouts  2.72 us (1%)
    pallas_call x1, Pallas kernels, per_device(): pl.pallas_call(finish_kernel, out_shape=tuple((jax.ShapeDtypeStruct(x.sha...  128 us
    pallas_call x1, Pallas kernels, per_device(): pl.pallas_call(functools.partial(kernel, ndp, nsec, blocks, listed, lent,...  81.6 us

profile of v3, /device:TPU:1, one launch (start us, length us, event | category | flops | bytes accessed | tf_op | source)
XLA Modules:
  0.0 213.2 jit_solution(10618052989856527202)
XLA Ops:
  0.6 1.4 copy.11.src_ref
  2.0 1.4 copy.12.lists_ref
  3.4 81.6 %shard_map.102 = (bf16[2048,256]{1,0:T(8,128)(2,1)}, f32[2048,256]{1,0:T(8,128)}, f32[2,256,256]{2,1,0:T(8,128)}, f32[2,256,256]{2,1,0:T(8,128)}) custom-call(s32[16,8]{1,0:T(8,128)} %copy.11.src_ref, s32[8,2,4]{2,1,0:T(2,128)} %copy.12.lists_ref, bf16[16,128,256]{2,1,0:T(8,128)(2,1)} %bitcast.9, bf16[128,128,128]{2,1,0:T(8,128)(2,1)} %bitcast.7, ...), custom_call_target="tpu_custom_call" | custom-call | tf_op jit(solution)/shard_map/pallas_call | solution.py:442
  84.9 128.3 %shard_map.103 = (bf16[2048,256]{1,0:T(8,128)(2,1)}, f32[2048,256]{1,0:T(8,128)}, f32[2,256,256]{2,1,0:T(8,128)}, f32[2,256,256]{2,1,0:T(8,128)}) custom-call(bf16[2048,256]{1,0:T(8,128)(2,1)} %get-tuple-element.12.h_in, f32[2048,256]{1,0:T(8,128)} %get-tuple-element.13.g_in, f32[2,256,256]{2,1,0:T(8,128)} %get-tuple-element.14.m_in, ...), custom_call_target="tpu_custom_call" | custom-call | tf_op jit(solution)/shard_map/pallas_call | solution.py:461

commit v4 on v3

--- a/solution.py
+++ b/solution.py
@@ -86,7 +86,7 @@
         return h[...].reshape(rows, width)
 
     def lent_block(d, i):
-        return lists_ref[sec, d, i]
+        return lists_ref[d, i, sec]
 
     def send_lent(layer, make):
         copies = []
@@ -153,7 +153,7 @@
     @pl.loop(0, blocks)
     def _(b):
         base = b * listed
-        ids = [src_ref[b, k] for k in range(listed)]
+        ids = [src_ref[k, b] for k in range(listed)]
         for k in reversed(range(listed - 1)):
             later = least([(base + m, ids[m] - ids[k]) for m in range(k + 1, listed)])
             tiles[base + k] = tiles[base + k] + tiles[later]
@@ -186,15 +186,11 @@
         at = pl.ds(i * per_chunk, per_chunk)
         pre = chunk_of(pre0, i) + halo_part(i)
         h1[at] = layer_out(chunk_of(h0, i), pre).reshape(per_chunk, tile, width)
-        put_turned(sg_t, i, silu_grad(pre))
+        pre0[at] = silu_grad(pre).reshape(per_chunk, tile, width)
 
     own_messages(1, h1)
     own_pre(1, h1, pre1)
     loads[4].wait()
-
-    @pl.loop(0, chunks)
-    def _(i):
-        put_turned(g_t, i, g[chunk_rows(i), :])
 
     for c in sends:
         c.wait()
@@ -356,6 +352,12 @@
         return out
 
     sends = send_back(1)
+
+    @pl.loop(0, chunks)
+    def _(i):
+        put_turned(g_t, i, g[chunk_rows(i), :])
+        put_turned(sg_t, i, chunk_of(pre0, i))
+
     put_part(0, mm(dpre_t[...], all_of(h1)))
     own_back(1, h1)
     put_part(1, message_part(1, h1))
@@ -395,17 +397,11 @@
         c.wait()
 
 
-def finish_kernel(h_in, g_in, m_in, s_in, h_out, g_out, m_out, s_out, sems):
-    copies = []
-    for src, dst, pieces in ((g_in, g_out, 4), (h_in, h_out, 4), (m_in, m_out, 1), (s_in, s_out, 1)):
-        size = src.shape[0] // pieces
-        for p in range(pieces):
-            at = pl.ds(p * size, size)
-            c = pltpu.make_async_copy(src.at[at], dst.at[at], sems.at[len(copies)])
-            c.start()
-            copies.append(c)
-    for c in copies:
-        c.wait()
+def finish_kernel(h_in, g_in, m_in, s_in, h_out, g_out, m_out, s_out):
+    h_out[...] = h_in[...]
+    g_out[...] = g_in[...]
+    m_out[...] = m_in[...]
+    s_out[...] = s_in[...]
 
 
 def per_device(ndp, nsec, hits, tiles, sources, send_list, w_message, w_self, cotangent):
@@ -454,16 +450,20 @@
             collective_id=0, has_side_effects=True, vmem_limit_bytes=56 * 1024 * 1024
         ),
     )(
-        sources[0], send_list[0], hits[0].reshape(blocks, tile, width),
+        sources[0].T, send_list[0].transpose(1, 2, 0), hits[0].reshape(blocks, tile, width),
         tiles.reshape(blocks * listed, tile, tile), cotangent[0], w_message, w_self,
     )
+    wide = pl.BlockSpec((rows // 4, width), lambda i: (i, 0))
+    deep = pl.BlockSpec((LAYERS, width // 4, width), lambda i: (0, i, 0))
+    specs = [wide, wide, deep, deep]
     results = (hit_output, grad, message_total, self_total)
     hit_output, grad, message_total, self_total = pl.pallas_call(
         finish_kernel,
         out_shape=tuple(jax.ShapeDtypeStruct(x.shape, x.dtype) for x in results),
-        in_specs=[far] * 4,
-        out_specs=(far,) * 4,
-        scratch_shapes=[sem((10,))],
+        grid=(4,),
+        compiler_params=pltpu.CompilerParams(vmem_limit_bytes=56 * 1024 * 1024),
+        in_specs=specs,
+        out_specs=tuple(specs),
     )(*results)
     return (hit_output[None], grad[None], message_total, self_total)
 

time: 214 us -> 87.9 us (0.41)
  Pallas kernels: 210 us -> 87 us
  local copies, waits for them, and re-layouts: 2.72 us -> 0 us
    pallas_call x1, Pallas kernels: 128 us -> 4.65 us  [per_device(): pl.pallas_call(finish_kernel, out_shape=tuple((jax.ShapeDtypeStruct(x.sha...]
    squeeze x2 -> x0, local copies, waits for them, and re-layouts: 2.72 us -> none  [the longest x1 1.36 us: per_device(): send_list[0]]
where the time goes in v4:
time: 87.9 us; the launch traced here: 87.7 us
  Pallas kernels  87 us (99%)
    pallas_call x1, Pallas kernels, per_device(): pl.pallas_call(functools.partial(kernel, ndp, nsec, blocks, listed, lent,...  82.4 us
    pallas_call x1, Pallas kernels, per_device(): pl.pallas_call(finish_kernel, out_shape=tuple((jax.ShapeDtypeStruct(x.sha...  4.65 us

profile of v4, /device:TPU:1, one launch (start us, length us, event | category | flops | bytes accessed | tf_op | source)
XLA Modules:
  0.0 87.7 jit_solution(1593944098186197633)
XLA Ops:
  0.6 82.4 %shard_map.102 = (bf16[2048,256]{1,0:T(8,128)(2,1)}, f32[2048,256]{1,0:T(8,128)}, f32[2,256,256]{2,1,0:T(8,128)}, f32[2,256,256]{2,1,0:T(8,128)}) custom-call(s32[8,16]{1,0:T(8,128)} %bitcast.14, s32[2,4,8]{2,1,0:T(4,128)} %bitcast.15, bf16[16,128,256]{2,1,0:T(8,128)(2,1)} %bitcast.13, bf16[128,128,128]{2,1,0:T(8,128)(2,1)} %bitcast.11, ...), custom_call_target="tpu_custom_call" | custom-call | tf_op jit(solution)/shard_map/pallas_call | solution.py:438
  83.0 4.7 %shard_map.103 = (bf16[2048,256]{1,0:T(8,128)(2,1)}, f32[2048,256]{1,0:T(8,128)}, f32[2,256,256]{2,1,0:T(8,128)}, f32[2,256,256]{2,1,0:T(8,128)}) custom-call(bf16[2048,256]{1,0:T(8,128)(2,1)} %get-tuple-element.12.h_in, f32[2048,256]{1,0:T(8,128)} %get-tuple-element.13.g_in, f32[2,256,256]{2,1,0:T(8,128)} %get-tuple-element.14.m_in, ...), custom_call_target="tpu_custom_call" | custom-call | tf_op jit(solution)/shard_map/pallas_call | solution.py:460

commit v5 on v4

--- a/solution.py
+++ b/solution.py
@@ -26,7 +26,7 @@
 def kernel(
     ndp, nsec, blocks, listed, lent, tile, width, r1, r2,
     src_ref, lists_ref, hits_hbm, tiles_hbm, cot_hbm, wm_hbm, ws_hbm,
-    hit_out, grad_out, mg_out, sg_out,
+    hit_out, grad_out, last_out, sums_out,
     h0, h1, h2, tiles, g, wm_ref, ws_ref, pre0, pre1, msg, hmsg, a_own, a_halo, halo, lend,
     g_t, sg_t, dpre_t, dmsg_t, own_t, back_send, back_recv0, back_recv1,
     part, rs1, q1, rs2, r_own, g2, g1,
@@ -52,8 +52,7 @@
         pltpu.make_async_copy(ws_hbm, ws_ref, load_sem.at[3]),
         pltpu.make_async_copy(cot_hbm, g, load_sem.at[4]),
     ]
-    for c in loads:
-        c.start()
+    loads[0].start()
 
     barrier = pltpu.get_barrier_semaphore()
     for p in sec_peers:
@@ -129,6 +128,9 @@
             dst[:, at] = d[j * tile : (j + 1) * tile, :].T
 
     loads[0].wait()
+    loads[1].start()
+    loads[2].start()
+    loads[3].start()
     for d in range(2):
         lend[0, d] = jnp.concatenate([h0[lent_block(d, i)] for i in range(lent)], axis=0)
     pl.semaphore_wait(barrier, nsec - 1 + ndp - 1)
@@ -166,6 +168,7 @@
                 a_halo[b, :, o * tile : (o + 1) * tile] = val
 
     loads[3].wait()
+    loads[4].start()
     own_pre(0, h0, pre0)
     for c in sends:
         c.wait()
@@ -261,12 +264,12 @@
                     total = total + back_recv[layer][d, pos].astype(F32)
                 lent_sum.append(total)
             total = (own_t[:, c] + jnp.concatenate(lent_sum, axis=1)).astype(BF)
-            new = g_t[:, c] + mm(wm_ref[layer], total)
             if layer > 0:
+                new = g_t[:, c] + mm(wm_ref[layer], total)
                 g_t[:, c] = new
                 dpre_t[:, c] = (new * sg_t[:, c]).astype(BF)
             else:
-                g[c, :] = new.T
+                dmsg_t[:, c] = total
 
     bounds = ((0, 2), (2, 2))
 
@@ -371,6 +374,8 @@
     sends = send_back(0)
     put_part(2, mm(dpre_t[...], all_of(h0)))
     own_back(0, h0)
+    grad_store = pltpu.make_async_copy(g_t, grad_out, store_sem.at[1])
+    grad_store.start()
     put_part(3, message_part(0, h0))
     second = rs1_start(1)
     first = ag1_start(0, first)
@@ -378,30 +383,24 @@
     second = ag2_start(1, second)
     for c in sends:
         c.wait()
-    grad_stores = []
-    for part_i in range(2):
-        at = pl.ds(part_i * (rows // 2), rows // 2)
-        finish_back(0, part_i * chunks // 2, (part_i + 1) * chunks // 2)
-        c = pltpu.make_async_copy(g.at[at], grad_out.at[at], store_sem.at[1 + part_i])
-        c.start()
-        grad_stores.append(c)
+    finish_back(0, 0, chunks)
+    last_store = pltpu.make_async_copy(dmsg_t, last_out, store_sem.at[2])
+    last_store.start()
     second = ag1_start(1, second)
     for c in first + second:
         c.wait()
-    scale = 1.0 / (float(rows * ndp * nsec) ** 0.5)
-    for m, out, layer in ((0, sg_out, 1), (1, mg_out, 1), (2, sg_out, 0), (3, mg_out, 0)):
-        out[layer, :, :128] = g1[m, :width, :].astype(F32) * scale
-        out[layer, :, 128:] = g1[m, width:, :].astype(F32) * scale
-    hit_store.wait()
-    for c in grad_stores:
-        c.wait()
-
-
-def finish_kernel(h_in, g_in, m_in, s_in, h_out, g_out, m_out, s_out):
+    sums_store = pltpu.make_async_copy(g1, sums_out, store_sem.at[3])
+    sums_store.start()
+    for c in (hit_store, grad_store, last_store, sums_store):
+        c.wait()
+
+
+def finish_kernel(scale, h_in, g_in, last_in, sums_in, wm_ref, h_out, g_out, m_out, s_out):
     h_out[...] = h_in[...]
-    g_out[...] = g_in[...]
-    m_out[...] = m_in[...]
-    s_out[...] = s_in[...]
+    g_out[...] = (g_in[...] + mm(wm_ref[0], last_in[...])).T
+    for m, out, layer in ((0, s_out, 1), (1, m_out, 1), (2, s_out, 0), (3, m_out, 0)):
+        out[layer, :, :128] = sums_in[m, 0].astype(F32) * scale
+        out[layer, :, 128:] = sums_in[m, 1].astype(F32) * scale
 
 
 def per_device(ndp, nsec, hits, tiles, sources, send_list, w_message, w_self, cotangent):
@@ -427,24 +426,23 @@
         vmem((4, folded, 128), BF), vmem((ndp - 1, 4, r1, 128), BF), vmem((4, r1, 128), BF),
         vmem((nsec - 1, 4, r2, 128), BF), vmem((4, r2, 128), BF), vmem((4, r1, 128), BF),
         vmem((4, folded, 128), BF),
-        sem((5,)), sem((3,)), sem((LAYERS, 2)), sem((LAYERS, 2)),
+        sem((5,)), sem((4,)), sem((LAYERS, 2)), sem((LAYERS, 2)),
         sem((LAYERS, 2, lent // 2)), sem((LAYERS, 2, lent // 2)),
         sem((2, ndp - 1)), sem((2, ndp - 1)), sem((2, nsec - 1)), sem((2, nsec - 1)),
         sem((2, nsec - 1)), sem((2, nsec - 1)), sem((2, ndp - 1)), sem((2, ndp - 1)),
     ]
     flat = pl.BlockSpec(memory_space=pltpu.SMEM)
     far = pl.BlockSpec(memory_space=pl.ANY)
-    near = pl.BlockSpec(memory_space=pltpu.VMEM)
-    hit_output, grad, message_total, self_total = pl.pallas_call(
+    hit_rows, grad_t, last_t, sums = pl.pallas_call(
         functools.partial(kernel, ndp, nsec, blocks, listed, lent, tile, width, r1, r2),
         out_shape=(
             jax.ShapeDtypeStruct((rows, width), BF),
-            jax.ShapeDtypeStruct((rows, width), F32),
-            jax.ShapeDtypeStruct(w_message.shape, F32),
-            jax.ShapeDtypeStruct(w_self.shape, F32),
+            jax.ShapeDtypeStruct((width, rows), F32),
+            jax.ShapeDtypeStruct((width, rows), BF),
+            jax.ShapeDtypeStruct((4, folded, 128), BF),
         ),
         in_specs=[flat, flat, far, far, far, far, far],
-        out_specs=(far, far, near, near),
+        out_specs=(far, far, far, far),
         scratch_shapes=scratch,
         compiler_params=pltpu.CompilerParams(
             collective_id=0, has_side_effects=True, vmem_limit_bytes=56 * 1024 * 1024
@@ -453,18 +451,26 @@
         sources[0].T, send_list[0].transpose(1, 2, 0), hits[0].reshape(blocks, tile, width),
         tiles.reshape(blocks * listed, tile, tile), cotangent[0], w_message, w_self,
     )
-    wide = pl.BlockSpec((rows // 4, width), lambda i: (i, 0))
-    deep = pl.BlockSpec((LAYERS, width // 4, width), lambda i: (0, i, 0))
-    specs = [wide, wide, deep, deep]
-    results = (hit_output, grad, message_total, self_total)
+    steps = 4
+    wide = pl.BlockSpec((rows // steps, width), lambda i: (i, 0))
+    tall = pl.BlockSpec((width, rows // steps), lambda i: (0, i))
+    deep = pl.BlockSpec((LAYERS, width // steps, width), lambda i: (0, i, 0))
+    pair = pl.BlockSpec((4, 2, width // steps, 128), lambda i: (0, 0, i, 0))
+    whole = pl.BlockSpec(w_message.shape, lambda i: (0, 0, 0))
+    scale = 1.0 / (float(rows * ndp * nsec) ** 0.5)
     hit_output, grad, message_total, self_total = pl.pallas_call(
-        finish_kernel,
-        out_shape=tuple(jax.ShapeDtypeStruct(x.shape, x.dtype) for x in results),
-        grid=(4,),
+        functools.partial(finish_kernel, scale),
+        out_shape=(
+            jax.ShapeDtypeStruct((rows, width), BF),
+            jax.ShapeDtypeStruct((rows, width), F32),
+            jax.ShapeDtypeStruct(w_message.shape, F32),
+            jax.ShapeDtypeStruct(w_self.shape, F32),
+        ),
+        grid=(steps,),
         compiler_params=pltpu.CompilerParams(vmem_limit_bytes=56 * 1024 * 1024),
-        in_specs=specs,
-        out_specs=tuple(specs),
-    )(*results)
+        in_specs=[wide, tall, tall, pair, whole],
+        out_specs=(wide, wide, deep, deep),
+    )(hit_rows, grad_t, last_t, sums.reshape(4, 2, width, 128), w_message)
     return (hit_output[None], grad[None], message_total, self_total)
 
 

time: 87.9 us -> 88.6 us (level)
  no operation moved by 1% of the time
where the time goes in v5:
time: 88.6 us; the launch traced here: 88.3 us
  Pallas kernels  87.7 us (99%)
    pallas_call x1, Pallas kernels, per_device(): pl.pallas_call(functools.partial(kernel, ndp, nsec, blocks, listed, lent,...  82.3 us
    pallas_call x1, Pallas kernels, per_device(): pl.pallas_call(functools.partial(finish_kernel, scale), out_shape=(jax.Sh...  5.32 us

profile of v5, /device:TPU:1, one launch (start us, length us, event | category | flops | bytes accessed | tf_op | source)
XLA Modules:
  0.0 88.3 jit_solution(3394518588994041424)
XLA Ops:
  0.6 82.3 %shard_map.102 = (bf16[2048,256]{1,0:T(8,128)(2,1)}, f32[256,2048]{1,0:T(8,128)}, bf16[256,2048]{1,0:T(8,128)(2,1)}, bf16[4,512,128]{2,1,0:T(8,128)(2,1)}) custom-call(s32[8,16]{1,0:T(8,128)} %bitcast.16, s32[2,4,8]{2,1,0:T(4,128)} %bitcast.17, bf16[16,128,256]{2,1,0:T(8,128)(2,1)} %bitcast.14, bf16[128,128,128]{2,1,0:T(8,128)(2,1)} %bitcast.12, ...), custom_call_target="tpu_custom_call" | custom-call | tf_op jit(solution)/shard_map/pallas_call | solution.py:436
  83.0 5.3 %shard_map.103 = (bf16[2048,256]{1,0:T(8,128)(2,1)}, f32[2048,256]{1,0:T(8,128)}, f32[2,256,256]{2,1,0:T(8,128)}, f32[2,256,256]{2,1,0:T(8,128)}) custom-call(bf16[2048,256]{1,0:T(8,128)(2,1)} %get-tuple-element.12.h_in, f32[256,2048]{1,0:T(8,128)} %get-tuple-element.13.g_in, bf16[256,2048]{1,0:T(8,128)(2,1)} %get-tuple-element.14.last_in, ...), custom_call_target="tpu_custom_call" | custom-call | tf_op jit(solution)/shard_map/pallas_call | solution.py:461
